TPU v7x, 32 devices: a whole 2x2x4 slice. The times are simulated.
32 devices in a mesh: rep: 4 (over y, x), shard: 8 (over z, core).
Axes of the slice: x: 2, y: 2, z: 4, core: 2. Of those that a mesh axis runs over, the one named last changes fastest.
Arguments:
- tokens: bfloat16 [32768, 768], P(('rep', 'shard')), may hold values from -6 to 6
- cotangent: bfloat16 [32768, 768], P(('rep', 'shard')), may hold values from -6 to 6
- deletion: int32 [128, 256], P(('rep', 'shard')), may hold values 0 or 1
- lengths: int32 [128], P(('rep', 'shard')), may hold values from 64 to 256, as said below
- qkv_weight: float32 [768, 2304], P('shard'), may hold values from -0.21875 to 0.21875
- out_weight: float32 [768, 768], P('shard'), may hold values from -0.875 to 0.875
- up_weight: float32 [768, 3072], P('shard'), may hold values from -0.21875 to 0.21875
- down_weight: float32 [3072, 768], P('shard'), may hold values from -0.109375 to 0.109375
- vectors: float32 [12, 768], P(None, 'shard'), may hold values from -2 to 2
- qkv_first: float32 [768, 2304], P('shard'), may hold values from -192 to 192
- out_first: float32 [768, 768], P('shard'), may hold values from -192 to 192
- up_first: float32 [768, 3072], P('shard'), may hold values from -192 to 192
- down_first: float32 [3072, 768], P('shard'), may hold values from -192 to 192
- vector_first: float32 [12, 768], P(None, 'shard'), may hold values from -192 to 192
- qkv_second: float32 [768, 2304], P('shard'), may hold values from 10 to 100000
- out_second: float32 [768, 768], P('shard'), may hold values from 10 to 100000
- up_second: float32 [768, 3072], P('shard'), may hold values from 10 to 100000
- down_second: float32 [3072, 768], P('shard'), may hold values from 10 to 100000
- vector_second: float32 [12, 768], P(None, 'shard'), may hold values from 10 to 100000
Outputs:
- output: bfloat16 [32768, 768], P(('rep', 'shard'))
- token_grad: bfloat16 [32768, 768], P(('rep', 'shard'))
- qkv_grad: float32 [768, 2304], P('shard')
- out_grad: float32 [768, 768], P('shard')
- up_grad: float32 [768, 3072], P('shard')
- down_grad: float32 [3072, 768], P('shard')
- vector_grad: float32 [12, 768], P(None, 'shard')
- qkv_step: float32 [768, 2304], P('shard')
- out_step: float32 [768, 768], P('shard')
- up_step: float32 [768, 3072], P('shard')
- down_step: float32 [3072, 768], P('shard')
- vector_step: float32 [12, 768], P(None, 'shard')
- qkv_first_new: float32 [768, 2304], P('shard')
- out_first_new: float32 [768, 768], P('shard')
- up_first_new: float32 [768, 3072], P('shard')
- down_first_new: float32 [3072, 768], P('shard')
- vector_first_new: float32 [12, 768], P(None, 'shard')
Inputs may be any that keep to these rules, and one draw needn't show every extreme that they name: `lengths`: in every draw some crop has all 256 positions in use and another only 64.
All inputs are finite; a program needn't handle non-finite values. No bound on the sum of `deletion` on one device may be relied on, other than what follows from the above.
Results may differ from a plain program's by a relative error of at most 0.015.
The roundings to bfloat16 on the way count: a program that leaves them out, or rounds other values in their place, can miss the bound.
Values may be sent and summed in bfloat16 or wider, within the bound.
A program may use at most 256 MiB of HBM per device.

v0:
```python
from functools import partial
import math

import jax
import jax.numpy as jnp
from jax import lax
from jax.sharding import PartitionSpec as P

D = 768
H = 12
FF = 3072
CROP = 256


norm_epsilon = 1e-06
decay_first = 0.9
decay_second = 0.999
correct_first = 1.0 - 2.6561398887587544e-05
correct_second = 0.0952078528862904
adam_epsilon = 1e-08


def layer_norm(hidden, gain_row, shift_row):
    average = jnp.mean(hidden, axis=-1, keepdims=True)
    centred = hidden - average
    variance = jnp.mean(centred * centred, axis=-1, keepdims=True)
    inverse_root = lax.rsqrt(variance + norm_epsilon)
    normed = centred * inverse_root
    return (normed * gain_row + shift_row, normed, inverse_root)


def norm_back(grad_output, normed, inverse_root, gain_row):
    grad_normed = grad_output * gain_row
    grad_input = inverse_root * (
        grad_normed
        - jnp.mean(grad_normed, axis=-1, keepdims=True)
        - normed * jnp.mean(grad_normed * normed, axis=-1, keepdims=True)
    )
    return (grad_input, jnp.sum(grad_output * normed, axis=0), jnp.sum(grad_output, axis=0))


def attend_block(pieces):
    packed, allowed_block = pieces
    score_scale = 1.0 / math.sqrt(packed.shape[-1])
    queries = packed[:, :, 0]
    keys_in = packed[:, :, 1]
    values = packed[:, :, 2]
    scores = (
        jnp.einsum("clhd,cmhd->chlm", queries, keys_in, preferred_element_type=jnp.float32)
        * score_scale
    )
    scores = jnp.where(allowed_block[:, None, None, :], scores, -1e30)
    row_top = jnp.max(scores, axis=-1, keepdims=True)
    log_totals = row_top + jnp.log(jnp.sum(jnp.exp(scores - row_top), axis=-1, keepdims=True))
    probs_low = jnp.exp(scores - log_totals).astype(jnp.bfloat16)
    mixed_rows = jnp.einsum(
        "chlm,cmhd->clhd", probs_low, values, preferred_element_type=jnp.float32
    )
    return (mixed_rows, log_totals[..., 0])


def attend_back(pieces):
    packed, allowed_block, log_totals, grad_mixed = pieces
    score_scale = 1.0 / math.sqrt(packed.shape[-1])
    queries = packed[:, :, 0]
    keys_in = packed[:, :, 1]
    values = packed[:, :, 2]
    scores = (
        jnp.einsum("clhd,cmhd->chlm", queries, keys_in, preferred_element_type=jnp.float32)
        * score_scale
    )
    scores = jnp.where(allowed_block[:, None, None, :], scores, -1e30)
    soft_probs = jnp.exp(scores - log_totals[..., None])
    grad_probs = jnp.einsum(
        "clhd,cmhd->chlm", grad_mixed, values, preferred_element_type=jnp.float32
    )
    grad_values = jnp.einsum(
        "chlm,clhd->cmhd",
        soft_probs.astype(jnp.bfloat16),
        grad_mixed,
        preferred_element_type=jnp.float32,
    )
    grad_scores = soft_probs * (
        grad_probs - jnp.sum(grad_probs * soft_probs, axis=-1, keepdims=True)
    )
    grad_low = grad_scores.astype(jnp.bfloat16)
    grad_queries = (
        jnp.einsum("chlm,cmhd->clhd", grad_low, keys_in, preferred_element_type=jnp.float32)
        * score_scale
    )
    grad_keys = (
        jnp.einsum("chlm,clhd->cmhd", grad_low, queries, preferred_element_type=jnp.float32)
        * score_scale
    )
    return jnp.stack([grad_queries, grad_keys, grad_values], axis=2)


def adam_update(gradient, first_moment, second_moment):
    first_new = decay_first * first_moment + (1.0 - decay_first) * gradient
    second_new = decay_second * second_moment + (1.0 - decay_second) * gradient * gradient
    step_dir = first_new / correct_first / (jnp.sqrt(second_new / correct_second) + adam_epsilon)
    return (step_dir, first_new)


def per_device(
    tokens,
    cotangent,
    deletion,
    lengths,
    qkv_weight,
    out_weight,
    up_weight,
    down_weight,
    vectors,
    qkv_first,
    out_first,
    up_first,
    down_first,
    vector_first,
    qkv_second,
    out_second,
    up_second,
    down_second,
    vector_second,
):
    crop_count = lengths.shape[0]
    head_size = D // H
    qkv_low = qkv_weight.astype(jnp.bfloat16)
    out_low = out_weight.astype(jnp.bfloat16)
    up_low = up_weight.astype(jnp.bfloat16)
    down_low = down_weight.astype(jnp.bfloat16)
    vector_low = vectors.astype(jnp.bfloat16)
    gathered = (
        lax.all_gather(qkv_low, "shard", axis=0, tiled=True),
        lax.all_gather(out_low, "shard", axis=0, tiled=True),
        lax.all_gather(up_low, "shard", axis=0, tiled=True),
        lax.all_gather(down_low, "shard", axis=0, tiled=True),
        lax.all_gather(vector_low, "shard", axis=1, tiled=True),
    )
    qkv_full, out_full, up_full, down_full, vector_full = gathered
    vector_float = vector_full.astype(jnp.float32)
    places = jnp.arange(CROP, dtype=jnp.int32)[None, :]
    allowed = ((deletion == 1) | (places == 0)) & (places < lengths[:, None])
    block_crops = math.gcd(crop_count, max(1, 512 // CROP))
    block_count = crop_count // block_crops
    allowed_blocks = allowed.reshape(block_count, block_crops, CROP)
    qkv_bias = jnp.concatenate([vector_float[0], jnp.zeros((D,), jnp.float32), vector_float[1]])
    qkv_act = (jnp.dot(tokens, qkv_full, preferred_element_type=jnp.float32) + qkv_bias).astype(
        jnp.bfloat16
    )
    packed = qkv_act.reshape(block_count, block_crops, CROP, 3, H, head_size)
    mixed_rows, log_totals = lax.map(attend_block, (packed, allowed_blocks))
    mixed_low = mixed_rows.reshape(crop_count * CROP, D).astype(jnp.bfloat16)
    branch = jnp.dot(mixed_low, out_full, preferred_element_type=jnp.float32) + vector_float[2]
    first_out, first_normed, first_root = layer_norm(
        tokens.astype(jnp.float32) + branch, vector_float[3], vector_float[4]
    )
    first_low = first_out.astype(jnp.bfloat16)
    inner_act = jnp.dot(first_low, up_full, preferred_element_type=jnp.float32) + vector_float[
        5:9
    ].reshape(FF)
    activated, gelu_back = jax.vjp(partial(jax.nn.gelu, approximate=False), inner_act)
    act_low = activated.astype(jnp.bfloat16)
    second = jnp.dot(act_low, down_full, preferred_element_type=jnp.float32) + vector_float[9]
    result, second_normed, second_root = layer_norm(
        first_out + second, vector_float[10], vector_float[11]
    )
    output = result.astype(jnp.bfloat16)
    back_set = (
        lax.all_gather(qkv_low, "shard", axis=0, tiled=True),
        lax.all_gather(out_low, "shard", axis=0, tiled=True),
        lax.all_gather(up_low, "shard", axis=0, tiled=True),
        lax.all_gather(down_low, "shard", axis=0, tiled=True),
        lax.all_gather(vector_low, "shard", axis=1, tiled=True),
    )
    qkv_back, out_back, up_back, down_back, vector_back = back_set
    vector_again = vector_back.astype(jnp.float32)
    keep_rows = allowed.reshape(crop_count * CROP).astype(jnp.float32)
    grad_result = cotangent.astype(jnp.float32) * keep_rows[:, None]
    grad_sum2, second_gain_grad, second_shift_grad = norm_back(
        grad_result, second_normed, second_root, vector_again[10]
    )
    grad_second = grad_sum2.astype(jnp.bfloat16)
    down_bias_grad = jnp.sum(grad_second, axis=0, dtype=jnp.float32)
    grad_down = jnp.einsum("tf,td->fd", act_low, grad_second, preferred_element_type=jnp.float32)
    grad_act = jnp.einsum("td,fd->tf", grad_second, down_back, preferred_element_type=jnp.float32)
    grad_inner = gelu_back(grad_act)[0].astype(jnp.bfloat16)
    up_bias_grad = jnp.sum(grad_inner, axis=0, dtype=jnp.float32)
    grad_up = jnp.einsum("td,tf->df", first_low, grad_inner, preferred_element_type=jnp.float32)
    grad_first = grad_sum2 + jnp.einsum(
        "tf,df->td", grad_inner, up_back, preferred_element_type=jnp.float32
    )
    grad_sum1, first_gain_grad, first_shift_grad = norm_back(
        grad_first, first_normed, first_root, vector_again[3]
    )
    grad_branch = grad_sum1.astype(jnp.bfloat16)
    out_bias_grad = jnp.sum(grad_branch, axis=0, dtype=jnp.float32)
    grad_out = jnp.einsum("td,te->de", mixed_low, grad_branch, preferred_element_type=jnp.float32)
    grad_mixed = jnp.einsum(
        "te,de->td", grad_branch, out_back, preferred_element_type=jnp.float32
    ).astype(jnp.bfloat16)
    grad_blocks = grad_mixed.reshape(block_count, block_crops, CROP, H, head_size)
    grad_packed = lax.map(attend_back, (packed, allowed_blocks, log_totals, grad_blocks))
    grad_qkv = grad_packed.reshape(crop_count * CROP, 3 * D).astype(jnp.bfloat16)
    bias_sums = jnp.sum(grad_qkv, axis=0, dtype=jnp.float32)
    grad_qkv_weight = jnp.einsum("td,te->de", tokens, grad_qkv, preferred_element_type=jnp.float32)
    token_grad = (
        grad_sum1 + jnp.einsum("te,de->td", grad_qkv, qkv_back, preferred_element_type=jnp.float32)
    ).astype(jnp.bfloat16)
    grad_vectors = jnp.concatenate(
        [
            jnp.stack(
                [
                    bias_sums[:D],
                    bias_sums[2 * D :],
                    out_bias_grad,
                    first_gain_grad,
                    first_shift_grad,
                ]
            ),
            up_bias_grad.reshape(4, D),
            jnp.stack([down_bias_grad, second_gain_grad, second_shift_grad]),
        ],
        axis=0,
    )
    group_sums = (
        lax.psum_scatter(grad_qkv_weight, "shard", scatter_dimension=0, tiled=True),
        lax.psum_scatter(grad_out, "shard", scatter_dimension=0, tiled=True),
        lax.psum_scatter(grad_up, "shard", scatter_dimension=0, tiled=True),
        lax.psum_scatter(grad_down, "shard", scatter_dimension=0, tiled=True),
        lax.psum_scatter(grad_vectors, "shard", scatter_dimension=1, tiled=True),
    )
    gradients = (
        lax.psum(group_sums[0].astype(jnp.bfloat16), "rep").astype(jnp.float32),
        lax.psum(group_sums[1].astype(jnp.bfloat16), "rep").astype(jnp.float32),
        lax.psum(group_sums[2].astype(jnp.bfloat16), "rep").astype(jnp.float32),
        lax.psum(group_sums[3].astype(jnp.bfloat16), "rep").astype(jnp.float32),
        lax.psum(group_sums[4].astype(jnp.bfloat16), "rep").astype(jnp.float32),
    )
    firsts = (qkv_first, out_first, up_first, down_first, vector_first)
    seconds = (qkv_second, out_second, up_second, down_second, vector_second)
    updated = [
        adam_update(gradient, first_moment, second_moment)
        for gradient, first_moment, second_moment in zip(gradients, firsts, seconds)
    ]
    return (
        output,
        token_grad,
        gradients[0],
        gradients[1],
        gradients[2],
        gradients[3],
        gradients[4],
        updated[0][0],
        updated[1][0],
        updated[2][0],
        updated[3][0],
        updated[4][0],
        updated[0][1],
        updated[1][1],
        updated[2][1],
        updated[3][1],
        updated[4][1],
    )


def solution(mesh):
    placed = (
        P(("rep", "shard"), None),
        P(("rep", "shard"), None),
        P(("rep", "shard"), None),
        P(("rep", "shard")),
        P("shard", None),
        P("shard", None),
        P("shard", None),
        P("shard", None),
        P(None, "shard"),
        P("shard", None),
        P("shard", None),
        P("shard", None),
        P("shard", None),
        P(None, "shard"),
        P("shard", None),
        P("shard", None),
        P("shard", None),
        P("shard", None),
        P(None, "shard"),
    )
    return jax.shard_map(
        per_device,
        mesh=mesh,
        in_specs=placed,
        out_specs=(
            P(("rep", "shard"), None),
            P(("rep", "shard"), None),
            P("shard", None),
            P("shard", None),
            P("shard", None),
            P("shard", None),
            P(None, "shard"),
            P("shard", None),
            P("shard", None),
            P("shard", None),
            P("shard", None),
            P(None, "shard"),
            P("shard", None),
            P("shard", None),
            P("shard", None),
            P("shard", None),
            P(None, "shard"),
        ),
        check_vma=False,
    )
```

profile of v0, /device:TPU:0, one launch (start us, length us, event | category | flops | bytes accessed | tf_op | source)
XLA Modules:
  0.0 704.1 jit_solution(15059409197622101852)
XLA Ops:
  7.2 2.1 convert_element_type.128
  9.4 1.8 convert_element_type.134
  12.2 2.3 convert_element_type.138
  14.6 15.8 %all-gather = bf16[8,96,12]{1,2,0:T(8,128)(2,1)S(1)} all-gather(bf16[1,96,12]{1,2,0:T(8,128)(2,1)S(1)} %convert_bitcast_fusion.1), channel_id=1, replica_groups=mesh['rep'=4,'shard'=8] {'shard'}, dimensions={0}, use_global_device_ids=true | all-gather | bytes 20736 | tf_op jit(solution)/shard_map/all_gather | solution.py:138
  31.3 1.7 copy.107
  33.5 1.6 copy.113
  35.1 19.5 %all-gather.6.cloned.1.call-done = bf16[768,2304]{1,0:T(8,128)(2,1)} async-done(((bf16[96,2304]{1,0:T(8,128)(2,1)}), bf16[768,2304]{1,0:T(8,128)(2,1)}) %all-gather.6.cloned.1.call-update) | async-done | bytes 3538960 | tf_op jit(solution)/shard_map/all_gather | solution.py:134
  54.6 7.5 %add_convert_fusion.1 = bf16[1024,2304]{1,0:T(8,128)(2,1)} fusion(bf16[1024,768]{1,0:T(8,128)(2,1)S(1)} %copy-done.7, bf16[768,2304]{1,0:T(8,128)(2,1)} %all-gather.6.cloned.1.call-done, f32[2304]{0:T(1024)S(1)} %pad_maximum_fusion), kind=kOutput, calls=%fused_computation.65 | convolution fusion | flops 3628597248 | bytes 9839616 | tf_op jit(solution)/shard_map/dot_general | solution.py:148
  62.1 6.6 copy.109
  68.8 8.9 %reshape.144 = bf16[2,2,256,3,12,64]{2,1,0,5,4,3:T(2,128)(2,1)} reshape(bf16[1024,2304]{0,1:T(8,128)(2,1)} %copy.109) | data formatting | bytes 9437184 | tf_op jit(solution)/shard_map/reshape | solution.py:151
  77.7 5.5 copy.110
  83.2 12.7 %while.22 = (s32[]{:T(128)}, bf16[2,2,256,12,64]{2,4,3,1,0:T(8,128)(2,1)S(1)}, f32[2,2,12,256]{3,2,1,0:T(8,128)S(1)}, bf16[2,2,256,3,12,64]{2,5,4,1,3,0:T(8,128)...) while((s32[]{:T(128)}, bf16[2,2,256,12,64]{2,4,3,1,0:T(8,128)(2,1)S(1)}, f32[2,2,12,256]{3,2,1,0:T(8,128)S(1)}, ...), condition=%wide.region_3.4_spmd, body=%wide.region_0.3_spmd.sunk | while | flops 419948544 | bytes 27766356 | solution.py:152
  83.2 1.8 dynamic-slice_bitcast_fusion.11
  89.5 1.8 dynamic-slice_bitcast_fusion.11
  95.9 1.6 copy.111
  97.5 2.3 convert_element_type.133
  99.8 3.9 fusion.72
  104.1 28.0 %all-gather.10.cloned.1.call-done = bf16[768,3072]{1,0:T(8,128)(2,1)} async-done(((bf16[96,3072]{1,0:T(8,128)(2,1)}), bf16[768,3072]{1,0:T(8,128)(2,1)}) %all-gather.10.cloned.1.call-update) | async-done | bytes 4718608 | tf_op jit(solution)/shard_map/all_gather | solution.py:136
  132.2 37.8 %multiply_convert_fusion.1 = (bf16[1024,3072]{1,0:T(8,128)(2,1)}, f32[1024,3072]{1,0:T(8,128)}, f32[1024,3072]{1,0:T(8,128)}) fusion(f32[3072]{0:T(1024)S(1)} %add.200, bf16[768,3072]{1,0:T(8,128)(2,1)} %all-gather.10.cloned.1.call-done, f32[1024,768]{0,1:T(8,128)S(1)} %get-tuple-element.266, f32[768]{0:T(1024)S(1)} %get-tuple-element.203, ...), kind=kOutput, calls=%fused_computation.50 | convolution fusion | flops 5043388416 | bytes 39348224 | tf_op jit(solution)/shard_map/dot_general | solution.py:159
  169.9 14.8 %all-gather.12.cloned.1.call-done = bf16[3072,768]{1,0:T(8,128)(2,1)} async-done(((bf16[384,768]{1,0:T(8,128)(2,1)}), bf16[3072,768]{1,0:T(8,128)(2,1)}) %all-gather.12.cloned.1.call-update) | async-done | bytes 4718608 | tf_op jit(solution)/shard_map/all_gather | solution.py:137
  184.8 9.4 %fusion.73 = (f32[1024]{0:T(1024)S(1)}, f32[1024,768]{0,1:T(8,128)S(1)}) fusion(f32[768]{0:T(1024)S(1)} %copy-done.39, bf16[1024,3072]{1,0:T(8,128)(2,1)} %get-tuple-element.254, bf16[3072,768]{1,0:T(8,128)(2,1)} %all-gather.12.cloned.1.call-done, f32[768]{0:T(1024)S(1)} %get-tuple-element.203, f32[768]{0:T(1024)S(1)} %get-tuple-element.204, ...), kind=kOutput, calls=%fused_computation.158 | convolution fusion | flops 4837342208 | bytes 17323008 | tf_op jit(solution)/shard_map/dot_general | solution.py:164
  195.6 2.1 multiply_reduce_fusion.1
  197.7 3.3 convert_reduce_fusion.2
  201.0 18.1 %convert_reduce_fusion = (f32[3072]{0:T(1024)}, bf16[1024,3072]{1,0:T(8,128)(2,1)}) fusion(f32[1024,3072]{1,0:T(8,128)} %get-tuple-element.255, bf16[1024,768]{0,1:T(8,128)(2,1)S(1)} %get-tuple-element.249, bf16[3072,768]{1,0:T(8,128)(2,1)} %all-gather.12.cloned.1.call-done, f32[1024,3072]{1,0:T(8,128)} %get-tuple-element.267, f32[3072]{0:T(1024)S(1)} %add.200), kind=kOutput, calls=%fused_computation.48 | convolution fusion | flops 4885312512 | bytes 37773312 | tf_op jit(solution)/shard_map/td,fd->tf/dot_general | solution.py:186
  219.1 11.2 %multiply_reduce_fusion.2 = (f32[768]{0:T(1024)S(1)}, f32[1024]{0:T(1024)S(1)}, f32[1024]{0:T(1024)S(1)}, f32[768]{0:T(1024)S(1)}, f32[1024,768]{0,1:T(8,128)S(1)}) fusion(f32[1024,768]{0,1:T(8,128)} %copy-done.1, f32[1024]{0:T(1024)S(1)} %add_rsqrt_fusion.1, f32[1024]{0:T(1024)S(1)} %broadcast_multiply_fusion.5, f32[768]{0:T(1024)S(1)} %get-tuple-element.204, ...), kind=kOutput, calls=%fused_computation.69 | convolution fusion | flops 4846776320 | bytes 22069248 | tf_op jit(solution)/shard_map/tf,df->td/dot_general | solution.py:190
  231.7 2.8 fusion.61
  234.5 3.9 convolution_convert_fusion
  238.4 1.7 copy.115
  241.4 25.9 %while.23 = (s32[]{:T(128)}, bf16[2,2,256,3,12,64]{2,5,4,1,3,0:T(8,128)(2,1)}, bf16[2,2,256,3,12,64]{2,5,4,1,3,0:T(8,128)(2,1)}, pred[2,2,256]{2,1,0:T(4,128)(4,...) while((s32[]{:T(128)}, ...), condition=%wide.region_14.15_spmd, body=%wide.region_12.14_spmd.sunk | while | flops 1038870528 | bytes 66244188 | solution.py:203
  241.7 1.8 dynamic-slice_bitcast_fusion.12
  245.2 2.3 multiply_reduce_fusion.9
  247.5 2.0 multiply_convert_fusion.3
  252.8 1.6 fusion.110
  254.4 1.8 dynamic-slice_bitcast_fusion.12
  258.0 2.3 multiply_reduce_fusion.9
  260.3 2.0 multiply_convert_fusion.3
  265.6 1.7 fusion.110
  267.3 9.4 %copy.118 = bf16[2,2,256,3,12,64]{2,1,0,5,4,3:T(2,128)(2,1)} copy(bf16[2,2,256,3,12,64]{2,5,4,1,3,0:T(8,128)(2,1)} %get-tuple-element.79) | data formatting | bytes 9437184 | tf_op jit(solution)/shard_map/convert_element_type | solution.py:204
  276.7 8.8 %convert_element_type.148 = bf16[1024,2304]{0,1:T(8,128)(2,1)} reshape(bf16[2,2,256,3,12,64]{2,1,0,5,4,3:T(2,128)(2,1)} %copy.118) | data formatting | bytes 9437184 | tf_op jit(solution)/shard_map/convert_element_type | solution.py:204
  285.6 8.3 %convolution_bitcast_fusion = f32[768,2304]{0,1:T(8,128)} fusion(bf16[1024,2304]{0,1:T(8,128)(2,1)} %convert_element_type.148, bf16[1024,768]{1,0:T(8,128)(2,1)S(1)} %copy-done.8), kind=kOutput, calls=%fused_computation.66 | convolution fusion | flops 3623878656 | bytes 13369344 | tf_op jit(solution)/shard_map/td,te->de/dot_general | solution.py:206
  293.9 8.0 %copy.134 = f32[768,2304]{1,0:T(8,128)} copy(f32[768,2304]{0,1:T(8,128)} %convolution_bitcast_fusion) | data formatting | bytes 14155776
  303.3 10.1 %fusion.74 = f32[3072,768]{1,0:T(8,128)} fusion(bf16[1024,3072]{1,0:T(8,128)(2,1)} %get-tuple-element.254, bf16[1024,768]{0,1:T(8,128)(2,1)S(1)} %copy-done.12), kind=kOutput, calls=%fused_computation.159 | convolution fusion | flops 4831838208 | bytes 17301504 | tf_op jit(solution)/shard_map/tf,td->fd/dot_general | solution.py:185
  313.5 1.9 copy-done.3
  315.4 10.5 %fusion.64 = f32[768,3072]{1,0:T(8,128)} fusion(bf16[1024,3072]{1,0:T(8,128)(2,1)} %get-tuple-element.272, f32[1024,768]{0,1:T(8,128)S(1)} %copy-done.3, f32[768]{0:T(1024)S(1)} %copy-done.38, f32[768]{0:T(1024)S(1)} %get-tuple-element.204, f32[1024]{0:T(1024)S(1)} %add_rsqrt_fusion.1, f32[1024]{0:T(1024)S(1)} %broadcast_multiply_fusion.5), kind=kOutput, calls=%fused_computation.154 | convolution fusion | flops 4835770368 | bytes 18888704 | tf_op jit(solution)/shard_map/td,tf->df/dot_general | solution.py:189
  326.0 3.0 convert_reduce_fusion.1
  330.5 1.6 convert_element_type.152
  332.2 45.9 %reduce-scatter.16.cloned.1.call-done = f32[96,2304]{1,0:T(8,128)} async-done(((f32[768,2304]{1,0:T(8,128)}), f32[96,2304]{1,0:T(8,128)}) %reduce-scatter.16.cloned.1.call-update) | async-done | bytes 884752
  378.1 2.2 copy.135
  380.3 98.0 %reduce-scatter.14.cloned.1.call-done = f32[384,768]{1,0:T(8,128)} async-done(((f32[3072,768]{1,0:T(8,128)}), f32[384,768]{1,0:T(8,128)}) %reduce-scatter.14.cloned.1.call-update) | async-done | bytes 1179664 | tf_op jit(solution)/shard_map/reduce_scatter | solution.py:230
  478.3 2.1 convert_element_type.156
  480.4 98.1 %reduce-scatter.12.cloned.1.call-done = f32[96,3072]{1,0:T(8,128)} async-done(((f32[768,3072]{1,0:T(8,128)}), f32[96,3072]{1,0:T(8,128)}) %reduce-scatter.12.cloned.1.call-update) | async-done | bytes 1179664 | tf_op jit(solution)/shard_map/reduce_scatter | solution.py:229
  578.5 2.2 convert_element_type.154
  581.1 2.6 copy.121
  583.6 9.3 %add_convert_fusion.2 = bf16[1024,768]{0,1:T(8,128)(2,1)} fusion(f32[1024,768]{0,1:T(8,128)} %copy-done.5, bf16[768,2304]{1,0:T(8,128)(2,1)} %all-gather.6.cloned.1.call-done, bf16[1024,2304]{0,1:T(8,128)(2,1)} %convert_element_type.148), kind=kOutput, calls=%fused_computation.71 | convolution fusion | flops 3625451520 | bytes 12976128 | tf_op jit(solution)/shard_map/te,de->td/dot_general | solution.py:208
  593.0 2.7 copy.123
  595.7 1.6 copy.122
  597.2 13.2 %reduce-scatter.18.cloned.1.call-done = f32[96,12]{1,0:T(8,128)} async-done(((f32[768,12]{1,0:T(8,128)}), f32[96,12]{1,0:T(8,128)}) %reduce-scatter.18.cloned.1.call-update) | async-done | bytes 4624
  611.3 10.2 %psum.39 = bf16[12,96]{1,0:T(8,128)(2,1)S(1)} all-reduce(bf16[12,96]{1,0:T(8,128)(2,1)S(1)} %copy.137), channel_id=1, replica_groups=mesh['rep'=4,'shard'=8] {'rep'}, use_global_device_ids=true, to_apply=%region_32.33 | all-reduce | flops 1152 | bytes 4608 | tf_op jit(solution)/shard_map/psum | solution.py:238
  622.1 58.8 %all-reduce.3.cloned.1.call-done = (bf16[96,2304]{0,1:T(8,128)(2,1)}, bf16[96,768]{1,0:T(8,128)(2,1)}, bf16[96,3072]{1,0:T(8,128)(2,1)}, bf16[384,768]{1,0:T(8,128)(2,1)}) async-done(((bf16[96,2304]{0,1:T(8,128)(2,1)}, bf16[96,768]{1,0:T(8,128)(2,1)}, bf16[96,3072]{1,0:T(8,128)(2,1)}, bf16[384,768]{1,0:T(8,128)(2,1)}), (bf16[96,2304]{0,1:T(8,128)(2,1)}, bf16[96,768]{1,0:T(8,128)(2,1)}, ...) | async-done | bytes 1769488 | tf_op jit(solution)/shard_map/psum | solution.py:234
  680.9 2.2 copy.124
  683.1 3.2 multiply_add_fusion.3
  686.3 2.7 copy.125
  690.3 3.3 fusion.48
  693.6 2.1 fusion.43
  (173 shorter events, 33.1 us)
Async XLA Ops:
  7.2 4.0 copy-start.17
  7.2 47.4 %all-gather.6.cloned.1.call-start = ((), (), s32[]{:S(2)}) async-start(), calls=%async_computation.5 | async-start | bytes 3981312 | tf_op jit(solution)/shard_map/all_gather | solution.py:134
  9.3 5.2 copy-start.34
  9.3 21.8 %copy-start.40 = (s32[4,256]{1,0:T(4,128)S(1)}, s32[4,256]{1,0:T(4,128)}, u32[]{:S(2)}) copy-start(s32[4,256]{1,0:T(4,128)} %param.25) | copy-start | bytes 12292
  9.3 21.8 %copy-start.41 = (s32[4]{0:T(128)S(1)}, s32[4]{0:T(128)}, u32[]{:S(2)}) copy-start(s32[4]{0:T(128)} %param.26) | copy-start | bytes 52
  9.3 21.9 %copy-start.7 = (bf16[1024,768]{1,0:T(8,128)(2,1)S(1)}, bf16[1024,768]{1,0:T(8,128)(2,1)}, u32[]{:S(2)}) copy-start(bf16[1024,768]{1,0:T(8,128)(2,1)} %param.23) | copy-start | bytes 4718596
  9.3 90.5 %all-gather.8.cloned.1.call-start = ((), (), s32[]{:S(2)}) async-start(), calls=%async_computation.6 | async-start | bytes 1327104 | tf_op jit(solution)/shard_map/all_gather | solution.py:135
  11.2 121.0 %all-gather.10.cloned.1.call-start = ((), (), s32[]{:S(2)}) async-start(), calls=%async_computation.7 | async-start | bytes 5308416 | tf_op jit(solution)/shard_map/all_gather | solution.py:136
  12.1 21.4 %copy-start.6 = (bf16[1024,768]{1,0:T(8,128)(2,1)S(1)}, bf16[1024,768]{1,0:T(8,128)(2,1)}, u32[]{:S(2)}) copy-start(bf16[1024,768]{1,0:T(8,128)(2,1)} %param.24) | copy-start | bytes 4718596
  12.1 172.7 %all-gather.12.cloned.1.call-start = ((), (), s32[]{:S(2)}) async-start(), calls=%async_computation.8 | async-start | bytes 5308416 | tf_op jit(solution)/shard_map/all_gather | solution.py:137
  14.5 316.1 %reduce-scatter.10.cloned.1.call-start = ((), (), s32[]{:S(2)}) async-start(), calls=%async_computation.9 | async-start | bytes 2654208 | tf_op jit(solution)/shard_map/reduce_scatter | solution.py:228
  31.1 153.7 %copy-start.37 = (f32[768]{0:T(1024)}, f32[768]{0:T(1024)S(1)}, u32[]{:S(2)}) copy-start(f32[768]{0:T(1024)S(1)} %get-tuple-element.203) | copy-start | bytes 9220
  77.7 5.5 copy-start.10
  95.8 4.0 copy-start.20
  95.8 4.0 copy-start.25
  103.7 81.1 %copy-start.1 = (f32[1024,768]{0,1:T(8,128)}, f32[1024,768]{0,1:T(8,128)S(1)}, u32[]{:S(2)}) copy-start(f32[1024,768]{0,1:T(8,128)S(1)} %get-tuple-element.266) | copy-start | bytes 9437188
  132.2 52.6 %copy-start.39 = (f32[768]{0:T(1024)S(1)}, f32[768]{0:T(1024)}, u32[]{:S(2)}) copy-start(f32[768]{0:T(1024)} %get-tuple-element.202) | copy-start | bytes 9220
  194.2 1.4 copy-start
  194.2 1.4 copy-start.27
  194.2 1.4 copy-start.28
  194.6 3.1 copy-start.29
  201.0 18.1 %copy-start.11 = (bf16[1024,768]{0,1:T(8,128)(2,1)}, bf16[1024,768]{0,1:T(8,128)(2,1)S(1)}, u32[]{:S(2)}) copy-start(bf16[1024,768]{0,1:T(8,128)(2,1)S(1)} %get-tuple-element.249) | copy-start | bytes 4718596
  219.1 11.2 %copy-start.2 = (f32[1024,768]{0,1:T(8,128)S(1)}, f32[1024,768]{0,1:T(8,128)}, u32[]{:S(2)}) copy-start(f32[1024,768]{0,1:T(8,128)} %copy-done.1) | copy-start | bytes 9437188
  230.3 1.4 copy-start.9
  231.4 3.1 copy-start.5
  240.1 1.3 copy-start.21
  240.1 1.3 copy-start.26
  241.4 136.7 %reduce-scatter.16.cloned.1.call-start = ((), (), s32[]{:S(2)}) async-start(), calls=%async_computation.12 | async-start | bytes 7962624
  276.7 8.8 %copy-start.8 = (bf16[1024,768]{1,0:T(8,128)(2,1)S(1)}, bf16[1024,768]{1,0:T(8,128)(2,1)}, u32[]{:S(2)}) copy-start(bf16[1024,768]{1,0:T(8,128)(2,1)} %param.23) | copy-start | bytes 4718596
  301.9 1.4 copy-start.12
  301.9 176.4 %reduce-scatter.14.cloned.1.call-start = ((), (), s32[]{:S(2)}) async-start(), calls=%async_computation.11 | async-start | bytes 10616832 | tf_op jit(solution)/shard_map/reduce_scatter | solution.py:230
  313.4 2.0 copy-start.3
  313.4 2.0 copy-start.38
  313.4 265.1 %reduce-scatter.12.cloned.1.call-start = ((), (), s32[]{:S(2)}) async-start(), calls=%async_computation.10 | async-start | bytes 10616832 | tf_op jit(solution)/shard_map/reduce_scatter | solution.py:229
  325.9 3.3 copy-start.33
  325.9 3.3 copy-start.32
  326.0 3.3 copy-start.31
  326.0 3.3 copy-start.30
  326.0 284.4 %reduce-scatter.18.cloned.1.call-start = ((), (), s32[]{:S(2)}) async-start(), calls=%async_computation.13 | async-start | bytes 442368
  330.5 350.4 %all-reduce.3.cloned.1.call-start = ((), (), s32[]{:S(2)}) async-start(), calls=%async_computation.14 | async-start | bytes 3833856 | tf_op jit(solution)/shard_map/psum | solution.py:234
  332.2 248.5 %copy-start.18 = (f32[96,2304]{1,0:T(8,128)S(1)}, f32[96,2304]{1,0:T(8,128)}, u32[]{:S(2)}) copy-start(f32[96,2304]{1,0:T(8,128)} %param.32) | copy-start | bytes 2654212
  593.0 2.7 copy-start.4
  593.0 28.5 %copy-start.35 = (f32[12,96]{1,0:T(8,128)S(1)}, f32[12,96]{1,0:T(8,128)}, u32[]{:S(2)}) copy-start(f32[12,96]{1,0:T(8,128)} %param.41) | copy-start | bytes 13828
  593.0 28.5 %copy-start.36 = (f32[12,96]{1,0:T(8,128)S(1)}, f32[12,96]{1,0:T(8,128)}, u32[]{:S(2)}) copy-start(f32[12,96]{1,0:T(8,128)} %param.36) | copy-start | bytes 13828
  686.3 4.0 copy-start.13
  686.3 4.0 copy-start.14
  690.3 3.3 copy-start.15
  690.3 3.3 copy-start.16
  690.3 3.3 copy-start.19
  693.6 2.2 copy-start.22
  693.6 2.2 copy-start.23
  693.6 2.1 copy-start.24
Sparse Core Ops, SparseCore 0:
  10.2 44.3 all-gather.5
  56.8 21.5 all-gather.7
  80.7 51.4 all-gather.9
  134.2 50.5 all-gather.11
  241.5 35.2 reduce-scatter.9
  302.0 76.0 reduce-scatter.15
  380.4 97.8 reduce-scatter.13
  480.6 97.8 reduce-scatter.11
  581.3 29.0 reduce-scatter.17
  615.3 65.5 all-reduce.2
where the time goes:
time: 715 us; the launch traced here: 704 us
  waiting for transfers between devices  376 us (53%)
  matrix products  152 us (21%)
  local copies, waits for them, and re-layouts  89.8 us (13%)
  other arithmetic  43.7 us (6%)
  blocking collectives  26 us (4%)
  between operations  15.2 us (2%)
    reduce_scatter x1, waiting for transfers between devices, per_device(): lax.psum_scatter(grad_up, 'shard', scatter_dimension=0, tiled=True)  98.1 us
    reduce_scatter x1, waiting for transfers between devices, per_device(): lax.psum_scatter(grad_down, 'shard', scatter_dimension=0, tiled=True)  98 us
    unnamed x12, waiting for transfers between devices  59.3 us
    psum x1, waiting for transfers between devices, per_device(): lax.psum(group_sums[0].astype(jnp.bfloat16), 'rep').astype(jnp.float32)  58.8 us
    dot_general x1, matrix products, per_device(): jnp.dot(first_low, up_full, preferred_element_type=jnp.float32)  37.8 us
    unnamed x98, local copies, waits for them, and re-layouts  33.9 us
    all_gather x1, waiting for transfers between devices, per_device(): lax.all_gather(up_low, 'shard', axis=0, tiled=True)  28 us
    all_gather x1, waiting for transfers between devices, per_device(): lax.all_gather(qkv_low, 'shard', axis=0, tiled=True)  19.5 us
  transfers between devices with their start and end apart: 10, of which 8 were waited for; matrix products, arithmetic and copies ran while one was open for 30% of the time, Pallas kernels for 0%

commit v1 on v0

v1 whole, which is shorter than its diff:
```python
import math
import jax, jax.numpy as jnp
from jax import lax
from jax.sharding import PartitionSpec as P
from jax.experimental import pallas as pl
from jax.experimental.pallas import tpu as pltpu
D=768; H=12; FF=3072; CROP=256; T=1024; NC=4
bf=jnp.bfloat16; f32=jnp.float32
EPS=1e-6
decay_first = 0.9
decay_second = 0.999
correct_first = 1.0 - 2.6561398887587544e-05
correct_second = 0.0952078528862904
adam_epsilon = 1e-08
def dg(a,b,ca,cb): return lax.dot_general(a,b,(((ca,),(cb,)),((),())),preferred_element_type=f32)
def rows_of(c): return pl.ds(pl.multiple_of(c*CROP,CROP),CROP)
def lanemean(v): return jnp.sum(v,axis=-1,keepdims=True)*(1.0/D)
def lanes(v,n): return jnp.concatenate([v]*n,axis=1)
OFF=dict(Q=0,K=768,V=1536,O=2304,U=3072,D=6144)

def gelu_parts(u):
    phi=jnp.exp(u*u*-0.5)*(1.0/math.sqrt(2*math.pi))
    cdf=0.5*(1.0+lax.erf(u*math.sqrt(0.5)))
    return u*cdf, cdf+u*phi

def kernel(tok_h,cot_h,allow_ref,vec_ref,w_h, out_h,tg_h,gw_h,vg_ref,
           W,x,qkv,pt,mixed,nrm1,root1,fl,act,gp,gs,gsec,cot,keep,sem):
    cps=[pltpu.make_async_copy(tok_h,x,sem.at[0]),pltpu.make_async_copy(cot_h,cot,sem.at[1]),pltpu.make_async_copy(w_h,W,sem.at[2])]
    for c in cps: c.start()
    mcol=allow_ref[...].T
    for c in range(NC):
        keep[c*CROP:(c+1)*CROP,:]=jnp.broadcast_to(mcol[:,c:c+1],(CROP,128))
    vg_ref[...]=jnp.zeros_like(vg_ref)
    for c in cps: c.wait()
    lane=lax.broadcasted_iota(jnp.int32,(CROP,128),1)
    low_half=lane<64
    def half(v,h): return jnp.where(low_half if h==0 else ~low_half, v, jnp.zeros_like(v))
    vrow=lambda r: vec_ref[r:r+1,:]
    @pl.loop(0,NC)
    def _(c):
      r=rows_of(c); xv=x[r,:]
      for b in range(3):
          y=dg(xv,W[b*D:(b+1)*D,:],1,0)
          if b==0: y=y+vrow(0)
          if b==2: y=y+vrow(1)
          qkv[r,b*D:(b+1)*D]=y.astype(bf)
    @pl.loop(0,NC)
    def _(c):
      r=rows_of(c)
      kp=lanes(keep[r,:],2)>0.5
      for p in range(6):
          q=qkv[r,p*128:(p+1)*128]*jnp.asarray(0.125,bf); k=qkv[r,D+p*128:D+(p+1)*128]; v=qkv[r,2*D+p*128:2*D+(p+1)*128]
          o=None
          for h in range(2):
              st=dg(k,half(q,h),1,1)
              st=jnp.where(kp,st,-1e30)
              e=jnp.exp(st-jnp.max(st,axis=0,keepdims=True))
              pr=(e*(1.0/jnp.sum(e,axis=0,keepdims=True))).astype(bf)
              pt[c,2*p+h]=pr
              t=dg(pr,half(v,h),0,0)
              o=t if o is None else o+t
          mixed[r,p*128:(p+1)*128]=o.astype(bf)
    @pl.loop(0,NC)
    def _(c):
      r=rows_of(c)
      h=x[r,:].astype(f32)+(dg(mixed[r,:],W[OFF['O']:OFF['O']+D,:],1,0)+vrow(2))
      h=h-lanemean(h)
      root=lax.rsqrt(lanemean(h*h)+EPS)
      n=h*root
      nrm1[r,:]=n
      root1[r,:]=jnp.broadcast_to(root,(CROP,128))
      fl[r,:]=(n*vrow(3)+vrow(4)).astype(bf)
    @pl.loop(0,NC)
    def _(c):
      r=rows_of(c); a=fl[r,:]
      for j in range(4):
          u=dg(a,W[OFF['U']+j*D:OFF['U']+(j+1)*D,:],1,0)+vrow(5+j)
          g,d=gelu_parts(u)
          act[r,j*D:(j+1)*D]=g.astype(bf)
          gp[r,j*D:(j+1)*D]=d.astype(bf)
    @pl.loop(0,NC)
    def _(c):
      r=rows_of(c)
      s=dg(act[r,:],W[OFF['D']:OFF['D']+FF,:],1,0)+vrow(9)
      h=nrm1[r,:]*vrow(3)+vrow(4)+s
      h=h-lanemean(h)
      root=lax.rsqrt(lanemean(h*h)+EPS)
      n=h*root
      G=cot[r,:].astype(f32)*lanes(keep[r,:],6)
      cot[r,:]=(n*vrow(10)+vrow(11)).astype(bf)
      vg_ref[10:11,:]+=jnp.sum(G*n,axis=0,keepdims=True)
      vg_ref[11:12,:]+=jnp.sum(G,axis=0,keepdims=True)
      dn=G*vrow(10)
      g2=root*(dn-lanemean(dn)-n*lanemean(dn*n))
      gs[r,:]=g2
      gb=g2.astype(bf)
      gsec[r,:]=gb
      vg_ref[9:10,:]+=jnp.sum(gb.astype(f32),axis=0,keepdims=True)
    oc=pltpu.make_async_copy(cot,out_h,sem.at[0]); oc.start()
    @pl.loop(0,NC)
    def _(c):
      r=rows_of(c); a=gsec[r,:]
      for j in range(4):
          ga=dg(a,W[OFF['D']+j*D:OFF['D']+(j+1)*D,:],1,1)
          gi=(ga*gp[r,j*D:(j+1)*D].astype(f32)).astype(bf)
          gp[r,j*D:(j+1)*D]=gi
          vg_ref[5+j:6+j,:]+=jnp.sum(gi.astype(f32),axis=0,keepdims=True)
    @pl.loop(0,6)
    def _(i):
      m=pl.ds(pl.multiple_of(i*512,512),512)
      W[pl.ds(pl.multiple_of(OFF['D']+i*512,512),512),:]=dg(act[:,m],gsec[...],0,0).astype(bf)
    @pl.loop(0,NC)
    def _(c):
      r=rows_of(c)
      G=gs[r,:]
      for j in range(4):
          G=G+dg(gp[r,j*D:(j+1)*D],W[OFF['U']+j*D:OFF['U']+(j+1)*D,:],1,1)
      n=nrm1[r,:]
      vg_ref[3:4,:]+=jnp.sum(G*n,axis=0,keepdims=True)
      vg_ref[4:5,:]+=jnp.sum(G,axis=0,keepdims=True)
      dn=G*vrow(3)
      g1=lanes(root1[r,:],6)*(dn-lanemean(dn)-n*lanemean(dn*n))
      gs[r,:]=g1
      gb=g1.astype(bf)
      gsec[r,:]=gb
      vg_ref[2:3,:]+=jnp.sum(gb.astype(f32),axis=0,keepdims=True)
    @pl.loop(0,4)
    def _(j):
      W[pl.ds(pl.multiple_of(OFF['U']+j*D,D),D),:]=dg(fl[...],gp[:,pl.ds(pl.multiple_of(j*D,D),D)],0,0).astype(bf)
    @pl.loop(0,NC)
    def _(c):
      r=rows_of(c)
      fl[r,:]=dg(gsec[r,:],W[OFF['O']:OFF['O']+D,:],1,1).astype(bf)
    @pl.loop(0,1)
    def _(i):
      W[OFF['O']:OFF['O']+D,:]=dg(mixed[...],gsec[...],0,0).astype(bf)
    @pl.loop(0,NC)
    def _(c):
      r=rows_of(c)
      for p in range(6):
          cq=slice(p*128,(p+1)*128); ck=slice(D+p*128,D+(p+1)*128); cv=slice(2*D+p*128,2*D+(p+1)*128)
          q=qkv[r,cq]*jnp.asarray(0.125,bf); k=qkv[r,ck]; v=qkv[r,cv]; do=fl[r,cq]
          dq=dk=dv=None
          for h in range(2):
              dom=half(do,h)
              dp=dg(v,dom,1,1)
              prb=pt[c,2*p+h]
              pr=prb.astype(f32)
              delta=jnp.sum(pr*dp,axis=0,keepdims=True)
              ds=(pr*(dp-delta)).astype(bf)
              tv=dg(prb,dom,1,0); tk=dg(ds,half(q,h),1,0); tq=dg(ds,half(k,h),0,0)
              dq,dk,dv=(tq,tk,tv) if dq is None else (dq+tq,dk+tk,dv+tv)
          act[r,cq]=(dq*0.125).astype(bf); act[r,ck]=dk.astype(bf); act[r,cv]=dv.astype(bf)
    @pl.loop(0,NC)
    def _(c):
      r=rows_of(c)
      G=gs[r,:]
      for b in range(3):
          g=act[r,b*D:(b+1)*D]
          G=G+dg(g,W[b*D:(b+1)*D,:],1,1)
          if b!=1:
              vg_ref[b//2:b//2+1,:]+=jnp.sum(g.astype(f32),axis=0,keepdims=True)
      gsec[r,:]=G.astype(bf)
    tc=pltpu.make_async_copy(gsec,tg_h,sem.at[1]); tc.start()
    @pl.loop(0,3)
    def _(j):
      W[pl.ds(pl.multiple_of(j*D,D),D),:]=dg(x[...],act[:,pl.ds(pl.multiple_of(j*D,D),D)],0,0).astype(bf)
    gc=pltpu.make_async_copy(W,gw_h,sem.at[2]); gc.start()
    for c in (oc,tc,gc): c.wait()

def layer(tok,cot,allow,vec,w):
    A=pl.BlockSpec(memory_space=pl.ANY); V=pl.BlockSpec(memory_space=pltpu.VMEM)
    VM=pltpu.VMEM
    return pl.pallas_call(kernel,
        out_shape=[jax.ShapeDtypeStruct((T,D),bf),jax.ShapeDtypeStruct((T,D),bf),jax.ShapeDtypeStruct((12*D,D),bf),jax.ShapeDtypeStruct((16,D),f32)],
        in_specs=[A,A,V,V,A],out_specs=[A,A,A,V],
        scratch_shapes=[VM((12*D,D),bf),VM((T,D),bf),VM((T,3*D),bf),VM((NC,H,CROP,CROP),bf),VM((T,D),bf),VM((T,D),f32),VM((T,128),f32),VM((T,D),bf),
            VM((T,FF),bf),VM((T,FF),bf),VM((T,D),f32),VM((T,D),bf),VM((T,D),bf),VM((T,128),f32),pltpu.SemaphoreType.DMA((3,))],
        compiler_params=pltpu.CompilerParams(vmem_limit_bytes=63*2**20))(tok,cot,allow,vec,w)


def adam_update(gradient, first_moment, second_moment):
    first_new = decay_first * first_moment + (1.0 - decay_first) * gradient
    second_new = decay_second * second_moment + (1.0 - decay_second) * gradient * gradient
    step_dir = first_new / correct_first / (jnp.sqrt(second_new / correct_second) + adam_epsilon)
    return (step_dir, first_new)


def allowed_rows(deletion, lengths):
    places = jnp.arange(CROP, dtype=jnp.int32)[None, :]
    allowed = ((deletion == 1) | (places == 0)) & (places < lengths[:, None])
    return jnp.pad(allowed.astype(f32), ((0, 8 - NC), (0, 0)))


def finish(output, token_grad, gradients, firsts, seconds):
    updated = [adam_update(g, m, s) for g, m, s in zip(gradients, firsts, seconds)]
    return (
        (output, token_grad)
        + tuple(gradients)
        + tuple(u[0] for u in updated)
        + tuple(u[1] for u in updated)
    )


def per_device_plain(tokens, cotangent, deletion, lengths, qkv, out, up, down, vectors, *moments):
    firsts, seconds = moments[:5], moments[5:]
    blocks = [qkv[:, b * D : (b + 1) * D] for b in range(3)] + [out]
    blocks += [up[:, b * D : (b + 1) * D] for b in range(4)]
    square = lax.all_gather(jnp.stack(blocks).astype(bf), "shard", axis=1, tiled=True)
    tall = lax.all_gather(down.astype(bf), "shard", axis=0, tiled=True)
    vec = lax.all_gather(vectors.astype(bf), "shard", axis=1, tiled=True).astype(f32)
    weights = jnp.concatenate([square.reshape(8 * D, D), tall], axis=0)
    output, token_grad, grads, vector_grads = layer(
        tokens, cotangent, allowed_rows(deletion, lengths), jnp.pad(vec, ((0, 4), (0, 0))), weights
    )
    grads = grads.astype(f32)
    square = lax.psum_scatter(
        grads[: 8 * D].reshape(8, D, D), "shard", scatter_dimension=1, tiled=True
    )
    tall = lax.psum_scatter(grads[8 * D :], "shard", scatter_dimension=0, tiled=True)
    vec = lax.psum_scatter(vector_grads[:12], "shard", scatter_dimension=1, tiled=True)
    square, tall, vec = (
        lax.psum(g.astype(bf), "rep").astype(f32) for g in (square, tall, vec)
    )
    gradients = (
        jnp.concatenate([square[0], square[1], square[2]], axis=1),
        square[3],
        jnp.concatenate([square[4], square[5], square[6], square[7]], axis=1),
        tall,
        vec,
    )
    return finish(output, token_grad, gradients, firsts, seconds)


def solution(mesh):
    rows = P(("rep", "shard"), None)
    weights = (P("shard", None),) * 4 + (P(None, "shard"),)
    return jax.shard_map(
        per_device_plain,
        mesh=mesh,
        in_specs=(rows, rows, rows, P(("rep", "shard"))) + weights * 3,
        out_specs=(rows, rows) + weights * 3,
        check_vma=False,
    )
```

time: 715 us -> 680 us (0.951); the launches traced: 704 us -> 679 us
  matrix products: 152 us -> 0 us
  waiting for transfers between devices: 376 us -> 481 us
  Pallas kernels: 0 us -> 96.4 us
  local copies, waits for them, and re-layouts: 89.8 us -> 26.8 us
  other arithmetic: 43.7 us -> 34.4 us
    dot_general x26 -> x0, matrix products: 152 us -> none  [the longest x1 37.8 us: per_device(): jnp.dot(first_low, up_full, preferred_element_type=jnp.float32)]
    pallas_call x0 -> x1, Pallas kernels: none -> 96.4 us  [layer(): pl.pallas_call(kernel, out_shape=[jax.ShapeDtypeStruct((T, D), bf), jax.S...]
    reduce_scatter x3 -> x2, waiting for transfers between devices: 196 us -> 271 us  [the longest x1 186 us: per_device_plain(): lax.psum_scatter(grads[:8 * D].reshape(8, D, D), 'shard', scatter_dimensi...]
    all_gather x4 -> x2, waiting for transfers between devices: 62.4 us -> 126 us  [the longest x1 91.7 us: per_device_plain(): lax.all_gather(jnp.stack(blocks).astype(bf), 'shard', axis=1, tiled=True)]
    convert_element_type x7 -> x0, local copies, waits for them, and re-layouts: 30.6 us -> none  [the longest x2 18.2 us: per_device(): grad_packed.reshape(crop_count * CROP, 3 * D).astype(jnp.bfloat16)]
    unnamed x12 -> x7, waiting for transfers between devices: 59.3 us -> 29 us
    unnamed x98 -> x47, local copies, waits for them, and re-layouts: 33.9 us -> 8.39 us
    slice x3 -> x2, local copies, waits for them, and re-layouts: 0.64 us -> 18.3 us  [the longest x1 11.6 us: per_device_plain(): grads[:8 * D].reshape(8, D, D)]
  transfers between devices with their start and end apart: 10 -> 6, of which waited for: 8 -> 6; matrix products, arithmetic and copies ran while one was open for 30% -> 3% of each run, Pallas kernels for 0% -> 0%
where the time goes in v1:
time: 680 us; the launch traced here: 679 us
  waiting for transfers between devices  481 us (71%)
  Pallas kernels  96.4 us (14%)
  other arithmetic  34.4 us (5%)
  local copies, waits for them, and re-layouts  26.8 us (4%)
  blocking collectives  25.9 us (4%)
  between operations  14.4 us (2%)
    reduce_scatter x1, waiting for transfers between devices, per_device_plain(): lax.psum_scatter(grads[:8 * D].reshape(8, D, D), 'shard', scatter_dimensi...  186 us
    pallas_call x1, Pallas kernels, layer(): pl.pallas_call(kernel, out_shape=[jax.ShapeDtypeStruct((T, D), bf), jax.S...  96.4 us
    all_gather x1, waiting for transfers between devices, per_device_plain(): lax.all_gather(jnp.stack(blocks).astype(bf), 'shard', axis=1, tiled=True)  91.7 us
    reduce_scatter x1, waiting for transfers between devices, per_device_plain(): lax.psum_scatter(grads[8 * D:], 'shard', scatter_dimension=0, tiled=True)  84.6 us
    psum x1, waiting for transfers between devices, per_device_plain(): lax.psum(g.astype(bf), 'rep').astype(f32)  54.9 us
    all_gather x1, waiting for transfers between devices, per_device_plain(): tall = lax.all_gather(down.astype(bf), 'shard', axis=0, tiled=True)  34.6 us
    unnamed x7, waiting for transfers between devices  29 us
    concatenate x1, other arithmetic, per_device_plain(): weights = jnp.concatenate([square.reshape(8 * D, D), tall], axis=0)  16.9 us
  transfers between devices with their start and end apart: 6, of which 6 were waited for; matrix products, arithmetic and copies ran while one was open for 3% of the time, Pallas kernels for 0%

profile of v1, /device:TPU:0, one launch (start us, length us, event | category | flops | bytes accessed | tf_op | source)
XLA Modules:
  0.0 679.5 jit_solution(15771729139517647791)
XLA Ops:
  7.2 0.0 copy-start.6
  7.2 0.0 all-gather.6.cloned.1.call-start
  7.2 2.2 convert_element_type.35
  9.5 0.0 all-gather.6.cloned.1.call-update
  9.5 0.0 all-gather.4.cloned.1.call-start
  9.5 0.0 copy-done.6
  9.6 1.1 copy-done.5
  10.7 0.1 convert.35
  10.9 0.8 copy-done.12
  11.7 0.0 copy-start.14
  11.7 0.0 copy-start.17
  11.8 0.0 copy-start.18
  11.8 0.0 copy-start
  11.9 1.0 copy-done
  12.9 0.0 all-gather.4.cloned.1.call-update
  12.9 0.0 reduce-scatter.8.cloned.1.call-start
  12.9 0.0 copy-done.14
  13.0 15.8 %all-gather = bf16[8,96,12]{1,2,0:T(8,128)(2,1)S(1)} all-gather(bf16[1,96,12]{1,2,0:T(8,128)(2,1)S(1)} %convert_bitcast_fusion), channel_id=1, replica_groups=mesh['rep'=4,'shard'=8] {'shard'}, dimensions={0}, use_global_device_ids=true | all-gather | bytes 20736 | tf_op jit(solution)/shard_map/all_gather | solution.py:211
  28.7 0.1 reshape.49
  28.9 0.0 copy-done.17
  28.9 0.1 fusion.32
  28.9 0.6 pad_convert_fusion.1.allow_ref
  29.6 0.6 pad_convert_fusion.vec_ref
  30.2 34.6 %all-gather.6.cloned.1.call-done = bf16[3072,768]{1,0:T(8,128)(2,1)} async-done(((bf16[384,768]{1,0:T(8,128)(2,1)}), bf16[3072,768]{1,0:T(8,128)(2,1)}) %all-gather.6.cloned.1.call-update) | async-done | bytes 4718608 | tf_op jit(solution)/shard_map/all_gather | solution.py:210
  64.8 91.7 %all-gather.4.cloned.1.call-done = bf16[8,768,768]{2,1,0:T(8,128)(2,1)} async-done(((bf16[8,96,768]{2,1,0:T(8,128)(2,1)}), bf16[8,768,768]{2,1,0:T(8,128)(2,1)}) %all-gather.4.cloned.1.call-update) | async-done | bytes 9437200 | tf_op jit(solution)/shard_map/all_gather | solution.py:209
  156.5 16.9 %pad_maximum_fusion.w_h = bf16[9216,768]{1,0:T(8,128)(2,1)} fusion(bf16[3072,768]{1,0:T(8,128)(2,1)} %all-gather.6.cloned.1.call-done, bf16[6144,768]{1,0:T(8,128)(2,1)} %bitcast.60), kind=kLoop, calls=%fused_computation | loop fusion | flops 28311552 | bytes 28311552 | tf_op jit(solution)/shard_map/concatenate | solution.py:212
  173.4 96.4 %shard_map.314 = (bf16[1024,768]{1,0:T(8,128)(2,1)}, bf16[1024,768]{1,0:T(8,128)(2,1)}, bf16[9216,768]{1,0:T(8,128)(2,1)}, f32[16,768]{1,0:T(8,128)}) custom-call(bf16[1024,768]{1,0:T(8,128)(2,1)} %tok_h.1, bf16[1024,768]{1,0:T(8,128)(2,1)} %cot_h.1, f32[8,256]{1,0:T(8,128)} %pad_convert_fusion.1.allow_ref, f32[16,768]{1,0:T(8,128)} %pad_convert_fusion.vec_ref, ...), custom_call_target="tpu_custom_call" | custom-call | tf_op jit(solution)/shard_map/pallas_call | solution.py:174
  269.8 6.7 slice.95
  276.5 0.0 reduce-scatter.8.cloned.1.call-update
  276.5 0.0 reduce-scatter.6.cloned.1.call-start
  276.5 11.6 %slice.86 = f32[6144,768]{1,0:T(8,128)} slice(bf16[9216,768]{1,0:T(8,128)(2,1)} %get-tuple-element.23), slice={[0:6144], [0:768]} | slice | bytes 37748736 | tf_op jit(solution)/shard_map/slice | solution.py:218
  288.2 0.0 reduce-scatter.6.cloned.1.call-update
  288.2 0.0 reduce-scatter.10.cloned.1.call-start
  288.2 0.7 copy-done.13
  289.0 0.9 copy.38
  289.9 0.0 reduce-scatter.10.cloned.1.call-update
  289.9 0.0 all-reduce.5.cloned.1.call-start
  290.0 84.6 %reduce-scatter.8.cloned.1.call-done = f32[384,768]{1,0:T(8,128)} async-done(((f32[3072,768]{1,0:T(8,128)}), f32[384,768]{1,0:T(8,128)}) %reduce-scatter.8.cloned.1.call-update) | async-done | bytes 1179664 | tf_op jit(solution)/shard_map/reduce_scatter | solution.py:220
  374.6 2.1 convert_element_type.39
  376.7 186.4 %reduce-scatter.6.cloned.1.call-done = f32[8,96,768]{2,1,0:T(8,128)} async-done(((f32[8,768,768]{2,1,0:T(8,128)}), f32[8,96,768]{2,1,0:T(8,128)}) %reduce-scatter.6.cloned.1.call-update) | async-done | bytes 2359312 | tf_op jit(solution)/shard_map/reduce_scatter | solution.py:217
  563.1 2.8 convert_element_type.37
  566.0 0.0 all-reduce.5.cloned.1.call-update
  566.0 28.9 %reduce-scatter.10.cloned.1.call-done = f32[96,12]{1,0:T(8,128)} async-done(((f32[768,12]{1,0:T(8,128)}), f32[96,12]{1,0:T(8,128)}) %reduce-scatter.10.cloned.1.call-update) | async-done | bytes 4624
  594.9 0.9 copy.39
  595.7 10.2 %psum.23 = bf16[12,96]{1,0:T(8,128)(2,1)S(1)} all-reduce(bf16[12,96]{1,0:T(8,128)(2,1)S(1)} %copy.39), channel_id=1, replica_groups=mesh['rep'=4,'shard'=8] {'rep'}, use_global_device_ids=true, to_apply=%region_5.6 | all-reduce | flops 1152 | bytes 4608 | tf_op jit(solution)/shard_map/psum | solution.py:223
  605.9 0.6 fusion.31
  606.6 54.9 %all-reduce.5.cloned.1.call-done = (bf16[8,96,768]{2,1,0:T(8,128)(2,1)}, bf16[384,768]{1,0:T(8,128)(2,1)}) async-done(((bf16[8,96,768]{2,1,0:T(8,128)(2,1)}, bf16[384,768]{1,0:T(8,128)(2,1)}), (bf16[8,96,768]{2,1,0:T(8,128)(2,1)}, bf16[384,768]{1,0:T(8,128)(2,1)})) %all-reduce.5.cloned.1.call-update) | async-done | bytes 1769488 | tf_op jit(solution)/shard_map/psum | solution.py:223
  661.4 1.5 convert_element_type.38
  662.9 0.0 copy-start.10
  662.9 0.0 copy-start.11
  662.9 0.0 copy-start.2
  662.9 0.1 slice_bitcast_fusion.3
  663.1 0.8 copy-done.10
  663.9 0.1 copy-done.11
  664.0 1.0 fusion.19
  664.9 0.0 copy-done.2
  664.9 0.7 copy-done.1
  665.6 0.1 copy-done.9
  665.8 2.0 fusion.9
  667.8 0.1 copy-done.8
  667.9 1.7 fusion.14
  669.6 0.0 copy-done.3
  669.6 0.9 copy-done.4
  670.5 2.1 fusion.4
  (27 shorter events, 0.2 us)
Async XLA Ops:
  7.2 2.3 copy-start.6
  7.2 57.6 %all-gather.6.cloned.1.call-start = ((), (), s32[]{:S(2)}) async-start(), calls=%async_computation.4 | async-start | bytes 5308416 | tf_op jit(solution)/shard_map/all_gather | solution.py:210
  9.5 1.3 copy-start.5
  9.5 147.0 %all-gather.4.cloned.1.call-start = ((), (), s32[]{:S(2)}) async-start(), calls=%async_computation.3 | async-start | bytes 10616832 | tf_op jit(solution)/shard_map/all_gather | solution.py:209
  10.7 1.0 copy-start.12
  11.7 1.2 copy-start.14
  11.7 17.1 %copy-start.17 = (s32[4,256]{1,0:T(4,128)S(1)}, s32[4,256]{1,0:T(4,128)}, u32[]{:S(2)}) copy-start(s32[4,256]{1,0:T(4,128)} %param.21) | copy-start | bytes 12292
  11.8 17.1 %copy-start.18 = (s32[4]{0:T(128)S(1)}, s32[4]{0:T(128)}, u32[]{:S(2)}) copy-start(s32[4]{0:T(128)} %param.22) | copy-start | bytes 52
  11.8 1.0 copy-start
  12.9 361.7 %reduce-scatter.8.cloned.1.call-start = ((), (), s32[]{:S(2)}) async-start(), calls=%async_computation.6 | async-start | bytes 10616832 | tf_op jit(solution)/shard_map/reduce_scatter | solution.py:220
  276.5 286.6 %reduce-scatter.6.cloned.1.call-start = ((), (), s32[]{:S(2)}) async-start(), calls=%async_computation.5 | async-start | bytes 21233664 | tf_op jit(solution)/shard_map/reduce_scatter | solution.py:217
  288.2 0.8 copy-start.13
  288.2 306.7 %reduce-scatter.10.cloned.1.call-start = ((), (), s32[]{:S(2)}) async-start(), calls=%async_computation.7 | async-start | bytes 442368
  289.9 371.5 %all-reduce.5.cloned.1.call-start = ((), (), s32[]{:S(2)}) async-start(), calls=%async_computation.8 | async-start | bytes 3538944 | tf_op jit(solution)/shard_map/psum | solution.py:223
  566.0 40.0 %copy-start.15 = (f32[12,96]{1,0:T(8,128)S(1)}, f32[12,96]{1,0:T(8,128)}, u32[]{:S(2)}) copy-start(f32[12,96]{1,0:T(8,128)} %param.37) | copy-start | bytes 13828
  566.0 40.0 %copy-start.16 = (f32[12,96]{1,0:T(8,128)S(1)}, f32[12,96]{1,0:T(8,128)}, u32[]{:S(2)}) copy-start(f32[12,96]{1,0:T(8,128)} %param.32) | copy-start | bytes 13828
  662.9 1.0 copy-start.10
  662.9 1.0 copy-start.11
  662.9 2.0 copy-start.2
  664.0 1.7 copy-start.1
  664.0 1.8 copy-start.9
  665.8 2.0 copy-start.7
  665.8 2.1 copy-start.8
  667.9 1.7 copy-start.3
  667.9 2.6 copy-start.4
Sparse Core Ops, SparseCore 0:
  10.2 54.4 all-gather.5
  67.0 89.5 all-gather.3
  276.6 97.9 reduce-scatter.7
  376.8 186.3 reduce-scatter.5
  565.8 29.0 reduce-scatter.9
  598.9 62.5 all-reduce.4

commit v2 on v1

v2 whole, which is shorter than its diff:
```python
import functools
import math

import jax
import jax.numpy as jnp
from jax import lax
from jax.experimental import pallas as pl
from jax.experimental.pallas import tpu as pltpu
from jax.sharding import PartitionSpec as P

D = 768
H = 12
FF = 3072
CROP = 256
T = 1024
NC = 4
SUB = 96
bf = jnp.bfloat16
f32 = jnp.float32
MESH = pl.DeviceIdType.MESH

norm_epsilon = 1e-06
decay_first = 0.9
decay_second = 0.999
correct_first = 1.0 - 2.6561398887587544e-05
correct_second = 0.0952078528862904
adam_epsilon = 1e-08


def dg(a, b, ca, cb):
    return lax.dot_general(a, b, (((ca,), (cb,)), ((), ())), preferred_element_type=f32)


def rows_of(c):
    return pl.ds(pl.multiple_of(c * CROP, CROP), CROP)


def lane_mean(v):
    return jnp.sum(v, axis=-1, keepdims=True) * (1.0 / D)


def lanes(v, n):
    return jnp.concatenate([v] * n, axis=1)


def gelu_parts(u):
    density = jnp.exp(u * u * -0.5) * (1.0 / math.sqrt(2.0 * math.pi))
    cdf = 0.5 * (1.0 + lax.erf(u * math.sqrt(0.5)))
    return u * cdf, cdf + u * density


def crop_loop(body, after=None):
    @pl.loop(0, NC)
    def _(c):
        body(c)
        for k, steps in (after or {}).items():

            @pl.when(c == k)
            def _():
                for step in steps:
                    step()


class Links:
    def __init__(self, refs):
        self.__dict__.update(refs)
        r = lax.axis_index("rep")
        s = lax.axis_index("shard")
        self.y, self.x = r // 2, r % 2
        self.z, self.c = s // 2, s % 2
        self.r, self.s = r, s
        self.rx = self.y * 2 + 1 - self.x
        self.ry = (1 - self.y) * 2 + self.x
        self.rd = 3 - r
        self.others = [(self.z + d) % 4 for d in (1, 2, 3)]
        self.dev_core = (r, self.z * 2 + 1 - self.c)
        self.dev_x = (self.rx, s)
        self.dev_y = (self.ry, s)
        self.dev_d = (self.rd, s)
        self.dev_z = [(r, z * 2 + self.c) for z in self.others]
        self.x1, self.y1, self.c1 = 1 - self.x, 1 - self.y, 1 - self.c
        self.s1 = self.z * 2 + self.c1
        self.s_others = [z * 2 + self.c for z in self.others]
        self.s1_others = [z * 2 + self.c1 for z in self.others]
        self.count = 0
        self.sent = []

    def greet(self):
        barrier = pltpu.get_barrier_semaphore()
        partners = [self.dev_core, self.dev_x, self.dev_y, self.dev_d] + self.dev_z
        for device in partners:
            pl.semaphore_signal(barrier, inc=1, device_id=device, device_id_type=MESH)
        pl.semaphore_wait(barrier, len(partners))

    def slot(self):
        self.count += 1
        return self.count - 1

    def copy(self, src, dst, k, device):
        return pltpu.make_async_remote_copy(
            src_ref=src,
            dst_ref=dst,
            send_sem=self.send_sem.at[k],
            recv_sem=self.recv_sem.at[k],
            device_id=device,
            device_id_type=MESH,
        )

    def part(self, g, jy, jx, z, c):
        if g == 2:
            return self.wd.at[z, c, jy, jx]
        return self.ws.at[g, jy, jx, z, c]

    def plan_gather(self):
        self.ag = [
            dict(
                core=[self.slot() for _ in range(4)],
                zed=[self.slot() for _ in range(3)],
                px=[self.slot() for _ in range(3)],
                py=[self.slot() for _ in range(3)],
                relay=[self.slot() for _ in range(3)],
                sib=[[self.slot() for _ in range(3)] for _ in range(4)],
            )
            for _ in range(3)
        ]
        self.ag_vec = dict(
            core=self.slot(), zed=[self.slot() for _ in range(3)], sib=[self.slot() for _ in range(3)]
        )

    def send(self, src, dst, k, device, keep):
        def describe():
            return self.copy(src[0](*src[1:]), dst[0](*dst[1:]), k, device)

        describe().start()
        keep.append(describe)

    def at(self, name, *index):
        return getattr(self, name).at[index if len(index) > 1 else index[0]]

    def same(self, ref, k, device, keep):
        self.send(ref, ref, k, device, keep)

    def arrive(self, ref, k, device):
        self.copy(ref[0](*ref[1:]), ref[0](*ref[1:]), k, device).wait_recv()

    def gather_start(self, g):
        for j in range(4):
            self.same(
                (self.part, g, j // 2, j % 2, self.z, self.c), self.ag[g]["core"][j], self.dev_core, self.sent
            )
        own = (self.part, g, self.y, self.x, self.z, self.c)
        for d in range(3):
            self.same(own, self.ag[g]["zed"][d], self.dev_z[d], self.sent)
        if g == 0:
            block = (self.at, "vb", self.s)
            self.same(block, self.ag_vec["core"], self.dev_core, self.sent)
            for d in range(3):
                self.same(block, self.ag_vec["zed"][d], self.dev_z[d], self.sent)

    def x_first(self, g, d):
        return (d != 1) == (g != 1)

    def gather_plane(self, g):
        for d in range(3):
            z, k = self.others[d], 2 - d
            ref = (self.part, g, self.y, self.x, z, self.c)
            self.arrive(ref, self.ag[g]["zed"][k], self.dev_z[d])
            self.same(ref, self.ag[g]["px"][d], self.dev_x, self.sent)
            self.same(ref, self.ag[g]["py"][d], self.dev_y, self.sent)
            self.same(ref, self.ag[g]["sib"][0][d], self.dev_core, self.sent)
            if g == 0:
                block = (self.at, "vb", self.s_others[d])
                self.arrive(block, self.ag_vec["zed"][k], self.dev_z[d])
                self.same(block, self.ag_vec["sib"][d], self.dev_core, self.sent)

    def gather_relay(self, g):
        for d in range(3):
            z = self.others[d]
            ref_x = (self.part, g, self.y, self.x1, z, self.c)
            self.arrive(ref_x, self.ag[g]["px"][d], self.dev_x)
            if self.x_first(g, d):
                self.same(ref_x, self.ag[g]["relay"][d], self.dev_y, self.sent)
            self.same(ref_x, self.ag[g]["sib"][1][d], self.dev_core, self.sent)
            ref_y = (self.part, g, self.y1, self.x, z, self.c)
            self.arrive(ref_y, self.ag[g]["py"][d], self.dev_y)
            if not self.x_first(g, d):
                self.same(ref_y, self.ag[g]["relay"][d], self.dev_x, self.sent)
            self.same(ref_y, self.ag[g]["sib"][2][d], self.dev_core, self.sent)

    def gather_last(self, g):
        for d in range(3):
            ref = (self.part, g, self.y1, self.x1, self.others[d], self.c)
            self.arrive(ref, self.ag[g]["relay"][d], self.dev_y if self.x_first(g, d) else self.dev_x)
            self.same(ref, self.ag[g]["sib"][3][d], self.dev_core, self.sent)

    def gather_wait(self, g):
        c = self.c1
        for j in range(4):
            self.arrive((self.part, g, j // 2, j % 2, self.z, c), self.ag[g]["core"][j], self.dev_core)
        spots = [
            (self.y, self.x),
            (self.y, self.x1),
            (self.y1, self.x),
            (self.y1, self.x1),
        ]
        for j, (jy, jx) in enumerate(spots):
            for d in range(3):
                self.arrive((self.part, g, jy, jx, self.others[d], c), self.ag[g]["sib"][j][d], self.dev_core)
        if g == 0:
            self.arrive((self.at, "vb", self.s1), self.ag_vec["core"], self.dev_core)
            for d in range(3):
                self.arrive((self.at, "vb", self.s1_others[d]), self.ag_vec["sib"][d], self.dev_core)

    def gather_drain(self):
        for copy in self.sent:
            copy().wait_send()
        self.sent = []

    def plan_sum(self):
        self.rs = [
            dict(
                core=[self.slot() for _ in range(4)],
                one=[self.slot() for _ in range(4)],
                two=[self.slot() for _ in range(4)],
                zed=[self.slot() for _ in range(3)],
                plane=[self.slot() for _ in range(3)],
            )
            for _ in range(3)
        ]
        self.rs_vec = dict(
            core=self.slot(), one=self.slot(), two=self.slot(), zed=[self.slot() for _ in range(3)]
        )
        self.out = [[], [], []]

    def grads(self, g, z, c, jy=slice(None), jx=slice(None)):
        if g == 1:
            return self.ws.at[1, jy, jx, z, c]
        return self.wd.at[z, c, jy, jx]

    def credit(self, i, device):
        pl.semaphore_signal(self.credit_sem.at[i], inc=1, device_id=device, device_id_type=MESH)

    def spend(self, g, i):
        if g != 2:
            pl.semaphore_wait(self.credit_sem.at[i], 1)

    def add(self, ref, other):
        ref, other = ref[0](*ref[1:]), other[0](*other[1:])
        ref[...] = (ref[...].astype(f32) + other[...].astype(f32)).astype(bf)

    def sum_start(self, g):
        self.spend(g, 0)
        for z in range(4):
            self.send(
                (self.grads, g, z, self.c1), (self.at, "rc", z), self.rs[g]["core"][z], self.dev_core, self.out[g]
            )
        if g == 0:
            self.send((self.at, "vs", 0), (self.at, "vr", 0), self.rs_vec["core"], self.dev_core, self.out[g])

    def sum_one(self, g):
        y, x, c = self.y, self.x, self.c
        for z in range(4):
            mine, came = (self.grads, g, z, c), (self.at, "rc", z)
            self.arrive(came, self.rs[g]["core"][z], self.dev_core)
            self.add(mine, came)
            if z == 0:
                self.spend(g, 1)
                self.spend(g, 2)
            if z < 2:
                self.send((self.grads, g, z, c, slice(None), self.x1), (self.at, "r1", z), self.rs[g]["one"][z], self.dev_x, self.out[g])
            else:
                self.send((self.grads, g, z, c, self.y1), (self.at, "r1", z), self.rs[g]["one"][z], self.dev_y, self.out[g])
        if g != 0:
            self.credit(0, self.dev_core)
        else:
            self.arrive((self.at, "vr", 0), self.rs_vec["core"], self.dev_core)
            self.vs[1] = self.vs[0] + self.vr[0]
            self.send((self.at, "vs", 1), (self.at, "vr", 1), self.rs_vec["one"], self.dev_x, self.out[g])

    def sum_two(self, g):
        y, x, c = self.y, self.x, self.c
        for z in range(4):
            came = (self.at, "r1", z)
            self.arrive(came, self.rs[g]["one"][z], self.dev_x if z < 2 else self.dev_y)
            self.add((self.grads, g, z, c, slice(None), x) if z < 2 else (self.grads, g, z, c, y), came)
            if z == 0:
                self.spend(g, 3)
                self.spend(g, 4)
            if z < 2:
                self.send((self.grads, g, z, c, self.y1, x), (self.at, "r2", z), self.rs[g]["two"][z], self.dev_y, self.out[g])
            else:
                self.send((self.grads, g, z, c, y, self.x1), (self.at, "r2", z), self.rs[g]["two"][z], self.dev_x, self.out[g])
        if g != 0:
            self.credit(1, self.dev_x)
            self.credit(2, self.dev_y)
        else:
            self.arrive((self.at, "vr", 1), self.rs_vec["one"], self.dev_x)
            self.vs[2] = self.vs[1] + self.vr[1]
            self.send((self.at, "vs", 2), (self.at, "vr", 2), self.rs_vec["two"], self.dev_y, self.out[g])

    def sum_zed(self, g):
        y, x, c = self.y, self.x, self.c
        for z in range(4):
            came = (self.at, "r2", z)
            self.arrive(came, self.rs[g]["two"][z], self.dev_y if z < 2 else self.dev_x)
            self.add((self.grads, g, z, c, y, x), came)
        for d in range(3):
            self.spend(g, 5 + d)
            self.send(
                (self.grads, g, self.others[d], c, y, x),
                (self.at, "rz", 2 - d),
                self.rs[g]["zed"][d],
                self.dev_z[d],
                self.out[g],
            )
        if g != 0:
            self.credit(3, self.dev_y)
            self.credit(4, self.dev_x)
        else:
            self.arrive((self.at, "vr", 2), self.rs_vec["two"], self.dev_y)
            self.vs[3] = self.vs[2] + self.vr[2]
            for d in range(3):
                self.send((self.at, "vs", 3), (self.at, "vr", 3 + 2 - d), self.rs_vec["zed"][d], self.dev_z[d], self.out[g])

    def sum_plane(self, g):
        total = self.grads(g, self.z, self.c, self.y, self.x)[...].astype(f32)
        for d in range(3):
            self.arrive((self.at, "rz", d), self.rs[g]["zed"][2 - d], self.dev_z[d])
            total = total + self.rz[d].astype(f32)
        own = (self.at, "gt", g, self.r)
        self.gt[g, self.r] = total.astype(bf)
        for k, device in enumerate((self.dev_x, self.dev_y, self.dev_d)):
            self.send(own, own, self.rs[g]["plane"][k], device, self.out[g])
        if g != 0:
            for d in range(3):
                self.credit(5 + 2 - d, self.dev_z[d])
        else:
            vec = self.vs[3]
            for d in range(3):
                self.arrive((self.at, "vr", 3 + d), self.rs_vec["zed"][2 - d], self.dev_z[d])
                vec = vec + self.vr[3 + d]
            self.vec_total[...] = vec

    def sum_wait(self, g):
        for k, (r, device) in enumerate(((self.rx, self.dev_x), (self.ry, self.dev_y), (self.rd, self.dev_d))):
            self.arrive((self.at, "gt", g, r), self.rs[g]["plane"][k], device)

    def sum_drain(self, g):
        for copy in self.out[g]:
            copy().wait_send()
        self.out[g] = []


def layer_kernel(linked, *refs):
    if linked:
        (tok_h, cot_h, allow_ref, vec_in, qkv_h, out_h, up_h, down_h) = refs[:8]
        (y_h, tg_h, gt_h, vg_out) = refs[8:12]
        rest = refs[12:]
    else:
        (tok_h, cot_h, allow_ref, vec_in, ws_h, wd_h) = refs[:6]
        (y_h, tg_h, g0_h, g1_h, g2_h, vg_out) = refs[6:12]
        rest = refs[12:]
    (ws, wd, x, qkv, pt, mixed, nrm1, root1, fl, act, gp, gs, gsec, cot, keep, vec_ref, vg_ref, sem) = rest[:18]
    if linked:
        names = ("vb", "rc", "r1", "r2", "rz", "gt", "vs", "vr", "send_sem", "recv_sem", "credit_sem")
        net = Links(dict(zip(names, rest[18:]), ws=ws, wd=wd, vec_total=vg_out))
        net.plan_gather()
        net.plan_sum()

    cp_x = pltpu.make_async_copy(tok_h, x, sem.at[0])
    cp_cot = pltpu.make_async_copy(cot_h, cot, sem.at[1])
    lane = lax.broadcasted_iota(jnp.int32, (CROP, 128), 1)
    low_half = lane < 64

    def half(v, h):
        return jnp.where(low_half if h == 0 else ~low_half, v, jnp.zeros_like(v))

    def vrow(r):
        return vec_ref[r : r + 1, :]

    def mat(g, j):
        if g == 2:
            return wd[j].reshape(D, D)
        return ws[g, j // 2, j % 2].reshape(D, D)

    def step(name, *a):
        return functools.partial(getattr(net, name), *a) if linked else (lambda: None)

    if linked:
        loads = []
        for j in range(4):
            src = qkv_h.at[:, j * D : (j + 1) * D] if j < 3 else out_h
            loads.append(pltpu.make_async_copy(src, gs.at[j * SUB : (j + 1) * SUB], sem.at[2 + j]))
        for j in range(4):
            loads.append(
                pltpu.make_async_copy(
                    up_h.at[:, j * D : (j + 1) * D], nrm1.at[j * SUB : (j + 1) * SUB], sem.at[6 + j]
                )
            )
        loads.append(pltpu.make_async_copy(down_h, gs.at[4 * SUB : 8 * SUB], sem.at[10]))
        for load in loads:
            load.start()
        cp_x.start()
        cp_cot.start()
        net.vb[net.s] = vec_in[...]
        for j in range(4):
            loads[j].wait()
            ws[0, j // 2, j % 2, net.z, net.c] = gs[j * SUB : (j + 1) * SUB].astype(bf)
        net.greet()
        net.gather_start(0)
        for j in range(4):
            loads[4 + j].wait()
            ws[1, j // 2, j % 2, net.z, net.c] = nrm1[j * SUB : (j + 1) * SUB].astype(bf)
        loads[8].wait()
        for j in range(4):
            wd[net.z, net.c, j // 2, j % 2] = gs[(4 + j) * SUB : (5 + j) * SUB].astype(bf)
    else:
        vec_ref[...] = vec_in[...]
        cp_ws = pltpu.make_async_copy(ws_h, ws, sem.at[2])
        cp_wd = pltpu.make_async_copy(wd_h, wd, sem.at[3])
        for copy in (cp_ws, cp_wd, cp_x, cp_cot):
            copy.start()
        cp_ws.wait()
        cp_wd.wait()
    mcol = allow_ref[...].T
    for c in range(NC):
        keep[c * CROP : (c + 1) * CROP, :] = jnp.broadcast_to(mcol[:, c : c + 1], (CROP, 128))
    vg_ref[...] = jnp.zeros_like(vg_ref)
    cp_x.wait()
    cp_cot.wait()
    if linked:
        net.gather_plane(0)
        net.gather_start(1)
        net.gather_relay(0)
        net.gather_last(0)
        net.gather_wait(0)
        row = lax.broadcasted_iota(jnp.int32, (128, D), 0)
        col = lax.broadcasted_iota(jnp.int32, (128, D), 1)
        vec = jnp.zeros((16, D), f32)
        for s in range(8):
            pick = ((col == row + s * SUB) & (row < SUB)).astype(f32).astype(bf)
            vec = vec + dg(net.vb[s], pick, 1, 0)
        vec_ref[...] = vec

    def body(c):
        r = rows_of(c)
        xv = x[r, :]
        for b in range(3):
            y = dg(xv, mat(0, b), 1, 0)
            if b == 0:
                y = y + vrow(0)
            if b == 2:
                y = y + vrow(1)
            qkv[r, b * D : (b + 1) * D] = y.astype(bf)

    crop_loop(body, {0: [step("gather_plane", 1)], 3: [step("gather_start", 2)]})

    def body(c):
        r = rows_of(c)
        kp = lanes(keep[r, :], 2) > 0.5
        for p in range(6):
            q = qkv[r, p * 128 : (p + 1) * 128] * jnp.asarray(0.125, bf)
            k = qkv[r, D + p * 128 : D + (p + 1) * 128]
            v = qkv[r, 2 * D + p * 128 : 2 * D + (p + 1) * 128]
            o = None
            for h in range(2):
                st = dg(k, half(q, h), 1, 1)
                st = jnp.where(kp, st, -1e30)
                e = jnp.exp(st - jnp.max(st, axis=0, keepdims=True))
                pr = (e * (1.0 / jnp.sum(e, axis=0, keepdims=True))).astype(bf)
                pt[c, 2 * p + h] = pr
                t = dg(pr, half(v, h), 0, 0)
                o = t if o is None else o + t
            mixed[r, p * 128 : (p + 1) * 128] = o.astype(bf)

    crop_loop(
        body,
        {
            0: [step("gather_relay", 1)],
            1: [step("gather_last", 1), step("gather_plane", 2)],
            3: [step("gather_relay", 2)],
        },
    )

    def body(c):
        r = rows_of(c)
        h = x[r, :].astype(f32) + (dg(mixed[r, :], mat(0, 3), 1, 0) + vrow(2))
        h = h - lane_mean(h)
        root = lax.rsqrt(lane_mean(h * h) + norm_epsilon)
        n = h * root
        nrm1[r, :] = n
        root1[r, :] = jnp.broadcast_to(root, (CROP, 128))
        fl[r, :] = (n * vrow(3) + vrow(4)).astype(bf)

    crop_loop(body)
    step("gather_last", 2)()
    step("gather_wait", 1)()

    def body(c):
        r = rows_of(c)
        a = fl[r, :]
        for j in range(4):
            u = dg(a, mat(1, j), 1, 0) + vrow(5 + j)
            g, d = gelu_parts(u)
            act[r, j * D : (j + 1) * D] = g.astype(bf)
            gp[r, j * D : (j + 1) * D] = d.astype(bf)

    crop_loop(body)
    step("gather_wait", 2)()

    def body(c):
        r = rows_of(c)
        s = dg(act[r, :], wd[...].reshape(FF, D), 1, 0) + vrow(9)
        h = nrm1[r, :] * vrow(3) + vrow(4) + s
        h = h - lane_mean(h)
        root = lax.rsqrt(lane_mean(h * h) + norm_epsilon)
        n = h * root
        G = cot[r, :].astype(f32) * lanes(keep[r, :], 6)
        cot[r, :] = (n * vrow(10) + vrow(11)).astype(bf)
        vg_ref[10:11, :] += jnp.sum(G * n, axis=0, keepdims=True)
        vg_ref[11:12, :] += jnp.sum(G, axis=0, keepdims=True)
        dn = G * vrow(10)
        g2 = root * (dn - lane_mean(dn) - n * lane_mean(dn * n))
        gs[r, :] = g2
        gb = g2.astype(bf)
        gsec[r, :] = gb
        vg_ref[9:10, :] += jnp.sum(gb.astype(f32), axis=0, keepdims=True)

    crop_loop(body)
    cp_y = pltpu.make_async_copy(cot, y_h, sem.at[0])
    cp_y.start()

    def body(c):
        r = rows_of(c)
        a = gsec[r, :]
        for j in range(4):
            ga = dg(a, mat(2, j), 1, 1)
            gi = (ga * gp[r, j * D : (j + 1) * D].astype(f32)).astype(bf)
            gp[r, j * D : (j + 1) * D] = gi
            vg_ref[5 + j : 6 + j, :] += jnp.sum(gi.astype(f32), axis=0, keepdims=True)

    crop_loop(body)
    step("gather_drain")()

    @pl.loop(0, 4)
    def _(i):
        m = pl.ds(pl.multiple_of(i * D, D), D)
        wd[i] = dg(act[:, m], gsec[...], 0, 0).astype(bf).reshape(2, 2, 2, SUB, D)

    step("sum_start", 2)()

    def body(c):
        r = rows_of(c)
        G = gs[r, :]
        for j in range(4):
            G = G + dg(gp[r, j * D : (j + 1) * D], mat(1, j), 1, 1)
        n = nrm1[r, :]
        vg_ref[3:4, :] += jnp.sum(G * n, axis=0, keepdims=True)
        vg_ref[4:5, :] += jnp.sum(G, axis=0, keepdims=True)
        dn = G * vrow(3)
        g1 = lanes(root1[r, :], 6) * (dn - lane_mean(dn) - n * lane_mean(dn * n))
        gs[r, :] = g1
        gb = g1.astype(bf)
        gsec[r, :] = gb
        vg_ref[2:3, :] += jnp.sum(gb.astype(f32), axis=0, keepdims=True)

    crop_loop(body, {2: [step("sum_one", 2)]})

    @pl.loop(0, 4)
    def _(j):
        g = gp[:, pl.ds(pl.multiple_of(j * D, D), D)]
        ws[1, j // 2, j % 2] = dg(fl[...], g, 0, 0).astype(bf).reshape(4, 2, SUB, D)

    step("sum_start", 1)()

    def body(c):
        r = rows_of(c)
        fl[r, :] = dg(gsec[r, :], mat(0, 3), 1, 1).astype(bf)

    crop_loop(body)
    step("sum_two", 2)()
    step("sum_one", 1)()

    def body(c):
        r = rows_of(c)
        for p in range(6):
            cq = slice(p * 128, (p + 1) * 128)
            ck = slice(D + p * 128, D + (p + 1) * 128)
            cv = slice(2 * D + p * 128, 2 * D + (p + 1) * 128)
            q = qkv[r, cq] * jnp.asarray(0.125, bf)
            k = qkv[r, ck]
            v = qkv[r, cv]
            do = fl[r, cq]
            dq = dk = dv = None
            for h in range(2):
                dom = half(do, h)
                dp = dg(v, dom, 1, 1)
                prb = pt[c, 2 * p + h]
                pr = prb.astype(f32)
                delta = jnp.sum(pr * dp, axis=0, keepdims=True)
                ds = (pr * (dp - delta)).astype(bf)
                tv = dg(prb, dom, 1, 0)
                tk = dg(ds, half(q, h), 1, 0)
                tq = dg(ds, half(k, h), 0, 0)
                dq, dk, dv = (tq, tk, tv) if dq is None else (dq + tq, dk + tk, dv + tv)
            dq = (dq * 0.125).astype(bf)
            dv = dv.astype(bf)
            act[r, cq] = dq
            act[r, ck] = dk.astype(bf)
            act[r, cv] = dv
            vg_ref[0:1, cq] += jnp.sum(dq.astype(f32), axis=0, keepdims=True)
            vg_ref[1:2, cq] += jnp.sum(dv.astype(f32), axis=0, keepdims=True)

    crop_loop(
        body,
        {
            0: [step("sum_zed", 2)],
            1: [step("sum_two", 1)],
            2: [step("sum_plane", 2)],
            3: [step("sum_zed", 1)],
        },
    )
    if linked:
        net.sum_drain(2)
        net.vs[0] = vg_ref[...]
    else:
        vg_out[...] = vg_ref[...]
        cp_g1 = pltpu.make_async_copy(ws.at[1], g1_h, sem.at[3])
        cp_g2 = pltpu.make_async_copy(wd, g2_h, sem.at[2])
        cp_g1.start()
        cp_g2.start()
        cp_g2.wait()

    for j in range(4):
        if j == 3:
            g = dg(mixed[...], gsec[...], 0, 0)
        else:
            g = dg(x[...], act[:, j * D : (j + 1) * D], 0, 0)
        wd[:, :, j // 2, j % 2] = g.astype(bf).reshape(4, 2, SUB, D)

    step("sum_start", 0)()

    def body(c):
        r = rows_of(c)
        G = gs[r, :]
        for b in range(3):
            G = G + dg(act[r, b * D : (b + 1) * D], mat(0, b), 1, 1)
        gsec[r, :] = G.astype(bf)

    crop_loop(body, {1: [step("sum_one", 0), step("sum_plane", 1)]})
    cp_tg = pltpu.make_async_copy(gsec, tg_h, sem.at[1])
    cp_tg.start()
    if linked:
        net.sum_two(0)
        net.sum_zed(0)
        net.sum_wait(2)
        net.sum_wait(1)
        net.sum_plane(0)
        net.sum_wait(0)
        cp_gt = pltpu.make_async_copy(net.gt, gt_h, sem.at[2])
        cp_gt.start()
        net.sum_drain(1)
        net.sum_drain(0)
        cp_gt.wait()
    else:
        cp_g0 = pltpu.make_async_copy(wd, g0_h, sem.at[2])
        cp_g0.start()
        cp_g0.wait()
        cp_g1.wait()
    cp_y.wait()
    cp_tg.wait()


WS = (2, 2, 2, 4, 2, SUB, D)
WD = (4, 2, 2, 2, SUB, D)


def layer(linked, *arrays):
    hbm = pl.BlockSpec(memory_space=pl.ANY)
    near = pl.BlockSpec(memory_space=pltpu.VMEM)
    VM = pltpu.VMEM
    shape = jax.ShapeDtypeStruct
    outs = [(shape((T, D), bf), hbm), (shape((T, D), bf), hbm)]
    if linked:
        outs += [(shape((3, 4, SUB, D), bf), hbm)]
    else:
        outs += [(shape(WD, bf), hbm), (shape(WS[1:], bf), hbm), (shape(WD, bf), hbm)]
    outs += [(shape((16, D), f32), near)]
    scratch = [
        VM(WS, bf),
        VM(WD, bf),
        VM((T, D), bf),
        VM((T, 3 * D), bf),
        VM((NC, H, CROP, CROP), bf),
        VM((T, D), bf),
        VM((T, D), f32),
        VM((T, 128), f32),
        VM((T, D), bf),
        VM((T, FF), bf),
        VM((T, FF), bf),
        VM((T, D), f32),
        VM((T, D), bf),
        VM((T, D), bf),
        VM((T, 128), f32),
        VM((16, D), f32),
        VM((16, D), f32),
        pltpu.SemaphoreType.DMA((11,)),
    ]
    params = dict(vmem_limit_bytes=63 * 2**20)
    if linked:
        transfers = 3 * (4 + 3 + 3 + 3 + 3 + 12) + 7 + 3 * (4 + 4 + 4 + 3 + 3) + 6
        scratch += [
            VM((8, 16, 128), bf),
            VM((4, 2, 2, SUB, D), bf),
            VM((4, 2, SUB, D), bf),
            VM((4, SUB, D), bf),
            VM((3, SUB, D), bf),
            VM((3, 4, SUB, D), bf),
            VM((4, 16, D), f32),
            VM((6, 16, D), f32),
            pltpu.SemaphoreType.DMA((transfers,)),
            pltpu.SemaphoreType.DMA((transfers,)),
            pltpu.SemaphoreType.REGULAR((8,)),
        ]
        params.update(collective_id=0, has_side_effects=True)
    return pl.pallas_call(
        functools.partial(layer_kernel, linked),
        out_shape=[o[0] for o in outs],
        in_specs=[hbm, hbm, near, near] + [hbm] * (len(arrays) - 4),
        out_specs=[o[1] for o in outs],
        scratch_shapes=scratch,
        compiler_params=pltpu.CompilerParams(**params),
    )(*arrays)


def adam_update(gradient, first_moment, second_moment):
    first_new = decay_first * first_moment + (1.0 - decay_first) * gradient
    second_new = decay_second * second_moment + (1.0 - decay_second) * gradient * gradient
    step_dir = first_new / correct_first / (jnp.sqrt(second_new / correct_second) + adam_epsilon)
    return (step_dir, first_new)


def allowed_rows(deletion, lengths):
    places = jnp.arange(CROP, dtype=jnp.int32)[None, :]
    allowed = ((deletion == 1) | (places == 0)) & (places < lengths[:, None])
    return jnp.pad(allowed.astype(f32), ((0, 8 - NC), (0, 0)))


def finish(output, token_grad, gradients, moments):
    updated = [adam_update(g, m, s) for g, m, s in zip(gradients, moments[:5], moments[5:])]
    return (
        (output, token_grad)
        + tuple(gradients)
        + tuple(u[0] for u in updated)
        + tuple(u[1] for u in updated)
    )


def side_by_side(blocks):
    return jnp.concatenate([blocks[j] for j in range(blocks.shape[0])], axis=1)


def per_device_linked(tokens, cotangent, deletion, lengths, qkv, out, up, down, vectors, *moments):
    vec = jnp.pad(vectors.astype(bf), ((0, 4), (0, 128 - vectors.shape[1])))
    output, token_grad, sums, vector_sums = layer(
        True, tokens, cotangent, allowed_rows(deletion, lengths), vec, qkv, out, up, down
    )
    sums = sums.astype(f32)
    width = vectors.shape[1]
    vec = lax.dynamic_slice(vector_sums, (0, lax.axis_index("shard") * width), (12, width))
    gradients = (
        side_by_side(sums[0, :3]),
        sums[0, 3],
        side_by_side(sums[1]),
        sums[2].reshape(4 * SUB, D),
        vec,
    )
    return finish(output, token_grad, gradients, moments)


def per_device_plain(tokens, cotangent, deletion, lengths, qkv, out, up, down, vectors, *moments):
    blocks = [qkv[:, b * D : (b + 1) * D] for b in range(3)] + [out]
    blocks += [up[:, b * D : (b + 1) * D] for b in range(4)]
    square = lax.all_gather(jnp.stack(blocks).astype(bf), "shard", axis=1, tiled=True)
    tall = lax.all_gather(down.astype(bf), "shard", axis=0, tiled=True)
    vec = lax.all_gather(vectors.astype(bf), "shard", axis=1, tiled=True).astype(f32)
    output, token_grad, g0, g1, g2, vec = layer(
        False,
        tokens,
        cotangent,
        allowed_rows(deletion, lengths),
        jnp.pad(vec, ((0, 4), (0, 0))),
        square.reshape(WS),
        tall.reshape(WD),
    )
    g0 = g0.transpose(2, 3, 0, 1, 4, 5).reshape(4, D, D)
    square = lax.psum_scatter(
        jnp.concatenate([g0, g1.reshape(4, D, D)]).astype(f32), "shard", scatter_dimension=1, tiled=True
    )
    tall = lax.psum_scatter(g2.reshape(FF, D).astype(f32), "shard", scatter_dimension=0, tiled=True)
    vec = lax.psum_scatter(vec[:12], "shard", scatter_dimension=1, tiled=True)
    square, tall, vec = (lax.psum(g.astype(bf), "rep").astype(f32) for g in (square, tall, vec))
    gradients = (side_by_side(square[:3]), square[3], side_by_side(square[4:]), tall, vec)
    return finish(output, token_grad, gradients, moments)


def solution(mesh):
    rows = P(("rep", "shard"), None)
    weights = (P("shard", None),) * 4 + (P(None, "shard"),)
    linked = mesh.shape["rep"] == 4 and mesh.shape["shard"] == 8
    return jax.shard_map(
        per_device_linked if linked else per_device_plain,
        mesh=mesh,
        in_specs=(rows, rows, rows, P(("rep", "shard"))) + weights * 3,
        out_specs=(rows, rows) + weights * 3,
        check_vma=False,
    )
```

time: 680 us -> 240 us (0.35)
  the two profiles are of different devices: /device:TPU:0 before, /device:TPU:28 now
where the time goes in v2:
time: 240 us; the launch traced here: 239 us
  Pallas kernels  219 us (91%)
  other arithmetic  12.7 us (5%)
  local copies, waits for them, and re-layouts  6.52 us (3%)
    pallas_call x1, Pallas kernels, layer(): pl.pallas_call(functools.partial(layer_kernel, linked), out_shape=[o[0] f...  219 us
    div x5, other arithmetic, adam_update(): first_new / correct_first  8.81 us
    unnamed x30, local copies, waits for them, and re-layouts  5.63 us

profile of v2, /device:TPU:28, one launch (start us, length us, event | category | flops | bytes accessed | tf_op | source)
XLA Modules:
  0.0 239.2 jit_solution(12961171931118772892)
XLA Ops:
  0.7 0.8 fusion.25
  1.4 0.6 pad_convert_fusion.refs_2_
  2.0 0.7 convert_element_type.11
  2.7 0.6 pad.12.refs_3_
  3.3 219.2 %shard_map.314 = (bf16[1024,768]{1,0:T(8,128)(2,1)}, bf16[1024,768]{1,0:T(8,128)(2,1)}, bf16[3,4,96,768]{3,2,1,0:T(8,128)(2,1)}, f32[16,768]{1,0:T(8,128)}) custom-call(bf16[1024,768]{1,0:T(8,128)(2,1)} %refs_0_.1, bf16[1024,768]{1,0:T(8,128)(2,1)} %refs_1_.1, f32[8,256]{1,0:T(8,128)} %pad_convert_fusion.refs_2_, bf16[16,128]{1,0:T(8,128)(2,1)} %pad.12.refs_3_, ...), custom_call_target="tpu_custom_call" | custom-call | tf_op jit(solution)/shard_map/pallas_call | solution.py:726
  222.6 1.8 convert_element_type.12
  224.4 0.0 copy-start.8
  224.4 0.0 copy-start.9
  224.4 0.2 slice_bitcast_fusion.3
  224.6 0.9 copy-done.8
  225.6 0.3 copy-done.9
  225.8 0.0 copy-start.10
  225.8 0.0 copy-start.11
  225.9 0.0 copy-start.5
  225.9 1.7 fusion.14
  227.5 0.0 copy-start.4
  227.5 0.0 copy-done.10
  227.5 0.0 copy-done.11
  227.5 1.0 fusion.19
  228.5 0.0 copy-done.5
  228.5 0.7 copy-done.4
  229.2 0.0 copy-start
  229.2 2.1 fusion.4
  231.4 0.0 copy-done
  231.4 0.0 copy-start.12
  231.4 0.0 copy-start.13
  231.4 0.0 copy-start.6
  231.4 0.0 copy-start.7
  231.4 0.1 slice.60
  231.5 0.0 copy-start.1
  231.5 0.6 copy-done.12
  232.1 0.0 copy-done.13
  232.1 1.9 fusion.24
  233.9 0.0 copy-done.6
  233.9 0.0 copy-done.7
  233.9 0.0 copy-start.3
  233.9 2.1 fusion.9
  236.1 0.0 copy-done.1
  236.1 0.0 copy-done.3
  236.1 0.0 copy-start.2
  236.1 1.1 copy.38
  237.2 0.8 copy-done.2
  238.1 1.1 copy.39
  (1 shorter events, 0.0 us)
Async XLA Ops:
  224.4 1.2 copy-start.8
  224.4 1.4 copy-start.9
  225.8 1.7 copy-start.10
  225.8 1.7 copy-start.11
  225.9 2.7 %copy-start.5 = (f32[96,3072]{1,0:T(8,128)S(1)}, f32[96,3072]{1,0:T(8,128)}, u32[]{:S(2)}) copy-start(f32[96,3072]{1,0:T(8,128)} %param.30) | copy-start | bytes 3538948
  227.5 1.7 copy-start.4
  229.2 2.2 copy-start
  231.4 0.7 copy-start.12
  231.4 0.7 copy-start.13
  231.4 2.6 %copy-start.6 = (f32[384,768]{1,0:T(8,128)S(1)}, f32[384,768]{1,0:T(8,128)}, u32[]{:S(2)}) copy-start(f32[384,768]{1,0:T(8,128)} %param.36) | copy-start | bytes 3538948
  231.4 2.6 %copy-start.7 = (f32[384,768]{1,0:T(8,128)S(1)}, f32[384,768]{1,0:T(8,128)}, u32[]{:S(2)}) copy-start(f32[384,768]{1,0:T(8,128)} %param.31) | copy-start | bytes 3538948
  231.5 4.6 %copy-start.1 = (f32[1,4,96,768]{3,2,1,0:T(8,128)}, f32[1,4,96,768]{3,2,1,0:T(8,128)S(1)}, u32[]{:S(2)}) copy-start(f32[1,4,96,768]{3,2,1,0:T(8,128)S(1)} %slice.60) | copy-start | bytes 3538948
  233.9 2.1 copy-start.3
  236.1 2.0 copy-start.2

commit v3 on v2

--- a/solution.py
+++ b/solution.py
@@ -33,6 +33,14 @@
 
 def rows_of(c):
     return pl.ds(pl.multiple_of(c * CROP, CROP), CROP)
+
+
+def third(t):
+    return slice(t * 256, (t + 1) * 256)
+
+
+def columns(g):
+    return third(g) if g < 3 else slice((g + 1) % 2 * 384, (g + 1) % 2 * 384 + 384)
 
 
 def lane_mean(v):
@@ -90,7 +98,9 @@
         partners = [self.dev_core, self.dev_x, self.dev_y, self.dev_d] + self.dev_z
         for device in partners:
             pl.semaphore_signal(barrier, inc=1, device_id=device, device_id_type=MESH)
-        pl.semaphore_wait(barrier, len(partners))
+
+    def greeted(self):
+        pl.semaphore_wait(pltpu.get_barrier_semaphore(), 7)
 
     def slot(self):
         self.count += 1
@@ -107,9 +117,9 @@
         )
 
     def part(self, g, jy, jx, z, c):
-        if g == 2:
-            return self.wd.at[z, c, jy, jx]
-        return self.ws.at[g, jy, jx, z, c]
+        if g > 4:
+            return self.wd.at[z, c, jy, jx, :, columns(g)]
+        return self.ws.at[g // 3, jy, jx, z, c, :, columns(g)]
 
     def plan_gather(self):
         self.ag = [
@@ -121,7 +131,7 @@
                 relay=[self.slot() for _ in range(3)],
                 sib=[[self.slot() for _ in range(3)] for _ in range(4)],
             )
-            for _ in range(3)
+            for _ in range(7)
         ]
         self.ag_vec = dict(
             core=self.slot(), zed=[self.slot() for _ in range(3)], sib=[self.slot() for _ in range(3)]
@@ -158,7 +168,7 @@
                 self.same(block, self.ag_vec["zed"][d], self.dev_z[d], self.sent)
 
     def x_first(self, g, d):
-        return (d != 1) == (g != 1)
+        return (d != 1) == (g % 2 == 0)
 
     def gather_plane(self, g):
         for d in range(3):
@@ -225,24 +235,33 @@
                 zed=[self.slot() for _ in range(3)],
                 plane=[self.slot() for _ in range(3)],
             )
-            for _ in range(3)
+            for _ in range(7)
         ]
         self.rs_vec = dict(
             core=self.slot(), one=self.slot(), two=self.slot(), zed=[self.slot() for _ in range(3)]
         )
-        self.out = [[], [], []]
+        self.out = [[] for _ in range(7)]
 
     def grads(self, g, z, c, jy=slice(None), jx=slice(None)):
-        if g == 1:
-            return self.ws.at[1, jy, jx, z, c]
-        return self.wd.at[z, c, jy, jx]
-
-    def credit(self, i, device):
-        pl.semaphore_signal(self.credit_sem.at[i], inc=1, device_id=device, device_id_type=MESH)
+        if g > 2:
+            return self.part(g, jy, jx, z, c)
+        return self.gp.at[jy, jx, pl.ds(pl.multiple_of((z * 2 + c) * SUB, SUB), SUB), third(g)]
+
+    def land(self, name, g, *index):
+        ref = getattr(self, name if name == "rc" or g > 2 else name + "t")
+        return ref.at[index + (slice(None),) * (len(ref.shape) - len(index) - 1) + (columns(g),)]
+
+    def total(self, g, r):
+        return self.gt.at[0 if g < 3 else (g - 1) // 2, r, :, columns(g)]
+
+    def credit(self, g, i, device):
+        if g > 4 or (g > 2 and i == 0):
+            pl.semaphore_signal(self.credit_sem.at[(g + 1) % 2 * 8 + i], inc=1, device_id=device, device_id_type=MESH)
 
     def spend(self, g, i):
-        if g != 2:
-            pl.semaphore_wait(self.credit_sem.at[i], 1)
+        for h in range(2):
+            if g == 3 + h or (g == 0 and i == 0):
+                pl.semaphore_wait(self.credit_sem.at[h * 8 + i], 1)
 
     def add(self, ref, other):
         ref, other = ref[0](*ref[1:]), other[0](*other[1:])
@@ -252,27 +271,26 @@
         self.spend(g, 0)
         for z in range(4):
             self.send(
-                (self.grads, g, z, self.c1), (self.at, "rc", z), self.rs[g]["core"][z], self.dev_core, self.out[g]
+                (self.grads, g, z, self.c1), (self.land, "rc", g, z), self.rs[g]["core"][z], self.dev_core, self.out[g]
             )
-        if g == 0:
+        if g == 2:
             self.send((self.at, "vs", 0), (self.at, "vr", 0), self.rs_vec["core"], self.dev_core, self.out[g])
 
     def sum_one(self, g):
         y, x, c = self.y, self.x, self.c
         for z in range(4):
-            mine, came = (self.grads, g, z, c), (self.at, "rc", z)
+            mine, came = (self.grads, g, z, c), (self.land, "rc", g, z)
             self.arrive(came, self.rs[g]["core"][z], self.dev_core)
             self.add(mine, came)
             if z == 0:
                 self.spend(g, 1)
                 self.spend(g, 2)
             if z < 2:
-                self.send((self.grads, g, z, c, slice(None), self.x1), (self.at, "r1", z), self.rs[g]["one"][z], self.dev_x, self.out[g])
+                self.send((self.grads, g, z, c, slice(None), self.x1), (self.land, "r1", g, z), self.rs[g]["one"][z], self.dev_x, self.out[g])
             else:
-                self.send((self.grads, g, z, c, self.y1), (self.at, "r1", z), self.rs[g]["one"][z], self.dev_y, self.out[g])
-        if g != 0:
-            self.credit(0, self.dev_core)
-        else:
+                self.send((self.grads, g, z, c, self.y1), (self.land, "r1", g, z), self.rs[g]["one"][z], self.dev_y, self.out[g])
+        self.credit(g, 0, self.dev_core)
+        if g == 2:
             self.arrive((self.at, "vr", 0), self.rs_vec["core"], self.dev_core)
             self.vs[1] = self.vs[0] + self.vr[0]
             self.send((self.at, "vs", 1), (self.at, "vr", 1), self.rs_vec["one"], self.dev_x, self.out[g])
@@ -280,20 +298,19 @@
     def sum_two(self, g):
         y, x, c = self.y, self.x, self.c
         for z in range(4):
-            came = (self.at, "r1", z)
+            came = (self.land, "r1", g, z)
             self.arrive(came, self.rs[g]["one"][z], self.dev_x if z < 2 else self.dev_y)
             self.add((self.grads, g, z, c, slice(None), x) if z < 2 else (self.grads, g, z, c, y), came)
             if z == 0:
                 self.spend(g, 3)
                 self.spend(g, 4)
             if z < 2:
-                self.send((self.grads, g, z, c, self.y1, x), (self.at, "r2", z), self.rs[g]["two"][z], self.dev_y, self.out[g])
+                self.send((self.grads, g, z, c, self.y1, x), (self.land, "r2", g, z), self.rs[g]["two"][z], self.dev_y, self.out[g])
             else:
-                self.send((self.grads, g, z, c, y, self.x1), (self.at, "r2", z), self.rs[g]["two"][z], self.dev_x, self.out[g])
-        if g != 0:
-            self.credit(1, self.dev_x)
-            self.credit(2, self.dev_y)
-        else:
+                self.send((self.grads, g, z, c, y, self.x1), (self.land, "r2", g, z), self.rs[g]["two"][z], self.dev_x, self.out[g])
+        self.credit(g, 1, self.dev_x)
+        self.credit(g, 2, self.dev_y)
+        if g == 2:
             self.arrive((self.at, "vr", 1), self.rs_vec["one"], self.dev_x)
             self.vs[2] = self.vs[1] + self.vr[1]
             self.send((self.at, "vs", 2), (self.at, "vr", 2), self.rs_vec["two"], self.dev_y, self.out[g])
@@ -301,22 +318,21 @@
     def sum_zed(self, g):
         y, x, c = self.y, self.x, self.c
         for z in range(4):
-            came = (self.at, "r2", z)
+            came = (self.land, "r2", g, z)
             self.arrive(came, self.rs[g]["two"][z], self.dev_y if z < 2 else self.dev_x)
             self.add((self.grads, g, z, c, y, x), came)
         for d in range(3):
             self.spend(g, 5 + d)
             self.send(
                 (self.grads, g, self.others[d], c, y, x),
-                (self.at, "rz", 2 - d),
+                (self.land, "rz", g, 2 - d),
                 self.rs[g]["zed"][d],
                 self.dev_z[d],
                 self.out[g],
             )
-        if g != 0:
-            self.credit(3, self.dev_y)
-            self.credit(4, self.dev_x)
-        else:
+        self.credit(g, 3, self.dev_y)
+        self.credit(g, 4, self.dev_x)
+        if g == 2:
             self.arrive((self.at, "vr", 2), self.rs_vec["two"], self.dev_y)
             self.vs[3] = self.vs[2] + self.vr[2]
             for d in range(3):
@@ -325,25 +341,24 @@
     def sum_plane(self, g):
         total = self.grads(g, self.z, self.c, self.y, self.x)[...].astype(f32)
         for d in range(3):
-            self.arrive((self.at, "rz", d), self.rs[g]["zed"][2 - d], self.dev_z[d])
-            total = total + self.rz[d].astype(f32)
-        own = (self.at, "gt", g, self.r)
-        self.gt[g, self.r] = total.astype(bf)
+            self.arrive((self.land, "rz", g, d), self.rs[g]["zed"][2 - d], self.dev_z[d])
+            total = total + self.land("rz", g, d)[...].astype(f32)
+        own = (self.total, g, self.r)
+        self.total(g, self.r)[...] = total.astype(bf)
         for k, device in enumerate((self.dev_x, self.dev_y, self.dev_d)):
             self.send(own, own, self.rs[g]["plane"][k], device, self.out[g])
-        if g != 0:
-            for d in range(3):
-                self.credit(5 + 2 - d, self.dev_z[d])
-        else:
+        for d in range(3):
+            self.credit(g, 5 + 2 - d, self.dev_z[d])
+        if g == 2:
             vec = self.vs[3]
             for d in range(3):
                 self.arrive((self.at, "vr", 3 + d), self.rs_vec["zed"][2 - d], self.dev_z[d])
                 vec = vec + self.vr[3 + d]
-            self.vec_total[...] = vec
+            self.vec_total[...] = pltpu.roll(vec, lax.rem(D - self.s * SUB, D), 1)[:, 0:128]
 
     def sum_wait(self, g):
         for k, (r, device) in enumerate(((self.rx, self.dev_x), (self.ry, self.dev_y), (self.rd, self.dev_d))):
-            self.arrive((self.at, "gt", g, r), self.rs[g]["plane"][k], device)
+            self.arrive((self.total, g, r), self.rs[g]["plane"][k], device)
 
     def sum_drain(self, g):
         for copy in self.out[g]:
@@ -353,17 +368,17 @@
 
 def layer_kernel(linked, *refs):
     if linked:
-        (tok_h, cot_h, allow_ref, vec_in, qkv_h, out_h, up_h, down_h) = refs[:8]
-        (y_h, tg_h, gt_h, vg_out) = refs[8:12]
-        rest = refs[12:]
+        (tok_h, cot_h, del_ref, len_ref, vec_in, qkv_h, out_h, up_h, down_h) = refs[:9]
+        (y_h, tg_h, t0_h, t1_h, t2_h, vg_out) = refs[9:15]
+        rest = refs[15:]
     else:
-        (tok_h, cot_h, allow_ref, vec_in, ws_h, wd_h) = refs[:6]
-        (y_h, tg_h, g0_h, g1_h, g2_h, vg_out) = refs[6:12]
-        rest = refs[12:]
+        (tok_h, cot_h, del_ref, len_ref, vec_in, ws_h, wd_h) = refs[:7]
+        (y_h, tg_h, g0_h, g1_h, g2_h, vg_out) = refs[7:13]
+        rest = refs[13:]
     (ws, wd, x, qkv, pt, mixed, nrm1, root1, fl, act, gp, gs, gsec, cot, keep, vec_ref, vg_ref, sem) = rest[:18]
     if linked:
-        names = ("vb", "rc", "r1", "r2", "rz", "gt", "vs", "vr", "send_sem", "recv_sem", "credit_sem")
-        net = Links(dict(zip(names, rest[18:]), ws=ws, wd=wd, vec_total=vg_out))
+        names = ("vb", "rc", "r1", "r2", "rz", "r1t", "r2t", "rzt", "gt", "vs", "vr", "send_sem", "recv_sem", "credit_sem")
+        net = Links(dict(zip(names, rest[18:]), ws=ws, wd=wd, gp=gp, vec_total=vg_out))
         net.plan_gather()
         net.plan_sum()
 
@@ -383,10 +398,14 @@
             return wd[j].reshape(D, D)
         return ws[g, j // 2, j % 2].reshape(D, D)
 
+    def mat_third(j, t):
+        return ws[0, j // 2, j % 2, :, :, :, third(t)].reshape(D, 256)
+
     def step(name, *a):
         return functools.partial(getattr(net, name), *a) if linked else (lambda: None)
 
     if linked:
+        net.greet()
         loads = []
         for j in range(4):
             src = qkv_h.at[:, j * D : (j + 1) * D] if j < 3 else out_h
@@ -402,11 +421,13 @@
             load.start()
         cp_x.start()
         cp_cot.start()
-        net.vb[net.s] = vec_in[...]
+        net.vs[0, :, 0:128] = jnp.zeros((16, 128), f32)
+        net.vs[0, 0 : vec_in.shape[0], 0 : vec_in.shape[1]] = vec_in[...]
+        net.vb[net.s] = net.vs[0, :, 0:128].astype(bf)
         for j in range(4):
             loads[j].wait()
             ws[0, j // 2, j % 2, net.z, net.c] = gs[j * SUB : (j + 1) * SUB].astype(bf)
-        net.greet()
+        net.greeted()
         net.gather_start(0)
         for j in range(4):
             loads[4 + j].wait()
@@ -422,9 +443,13 @@
             copy.start()
         cp_ws.wait()
         cp_wd.wait()
-    mcol = allow_ref[...].T
+    place = lax.broadcasted_iota(jnp.int32, (1, CROP), 1)
+    allowed = [
+        jnp.where(((del_ref[c : c + 1, :] == 1) | (place == 0)) & (place < len_ref[c]), 1.0, 0.0) for c in range(NC)
+    ]
+    mcol = jnp.concatenate(allowed * (8 // NC), axis=0).T
     for c in range(NC):
-        keep[c * CROP : (c + 1) * CROP, :] = jnp.broadcast_to(mcol[:, c : c + 1], (CROP, 128))
+        keep[c * CROP : (c + 1) * CROP, :] = jnp.broadcast_to(mcol[:, c : c + 1], (CROP, 128)).astype(bf)
     vg_ref[...] = jnp.zeros_like(vg_ref)
     cp_x.wait()
     cp_cot.wait()
@@ -432,6 +457,8 @@
         net.gather_plane(0)
         net.gather_start(1)
         net.gather_relay(0)
+        net.gather_plane(1)
+        net.gather_start(2)
         net.gather_last(0)
         net.gather_wait(0)
         row = lax.broadcasted_iota(jnp.int32, (128, D), 0)
@@ -442,44 +469,54 @@
             vec = vec + dg(net.vb[s], pick, 1, 0)
         vec_ref[...] = vec
 
-    def body(c):
+    def project(t, c):
         r = rows_of(c)
         xv = x[r, :]
         for b in range(3):
-            y = dg(xv, mat(0, b), 1, 0)
+            y = dg(xv, mat_third(b, t), 1, 0)
             if b == 0:
-                y = y + vrow(0)
+                y = y + vec_ref[0:1, third(t)]
             if b == 2:
-                y = y + vrow(1)
-            qkv[r, b * D : (b + 1) * D] = y.astype(bf)
-
-    crop_loop(body, {0: [step("gather_plane", 1)], 3: [step("gather_start", 2)]})
-
-    def body(c):
+                y = y + vec_ref[1:2, third(t)]
+            qkv[r, t * D + b * 256 : t * D + (b + 1) * 256] = y.astype(bf)
+
+    def attend(t, c):
         r = rows_of(c)
-        kp = lanes(keep[r, :], 2) > 0.5
-        for p in range(6):
-            q = qkv[r, p * 128 : (p + 1) * 128] * jnp.asarray(0.125, bf)
-            k = qkv[r, D + p * 128 : D + (p + 1) * 128]
-            v = qkv[r, 2 * D + p * 128 : 2 * D + (p + 1) * 128]
+        kp = lanes(keep[r, :].astype(f32), 2) > 0.5
+        for p in range(2):
+            q, k, v = (qkv[r, t * D + b * 256 + p * 128 : t * D + b * 256 + (p + 1) * 128] for b in range(3))
+            q = q * jnp.asarray(0.125, bf)
             o = None
             for h in range(2):
                 st = dg(k, half(q, h), 1, 1)
                 st = jnp.where(kp, st, -1e30)
                 e = jnp.exp(st - jnp.max(st, axis=0, keepdims=True))
                 pr = (e * (1.0 / jnp.sum(e, axis=0, keepdims=True))).astype(bf)
-                pt[c, 2 * p + h] = pr
-                t = dg(pr, half(v, h), 0, 0)
-                o = t if o is None else o + t
-            mixed[r, p * 128 : (p + 1) * 128] = o.astype(bf)
-
+                pt[c, 4 * t + 2 * p + h] = pr
+                w = dg(pr, half(v, h), 0, 0)
+                o = w if o is None else o + w
+            mixed[r, t * 256 + p * 128 : t * 256 + (p + 1) * 128] = o.astype(bf)
+
+    crop_loop(functools.partial(project, 0), {0: [step("gather_relay", 1), step("gather_plane", 2), step("gather_start", 3)]})
     crop_loop(
-        body,
+        functools.partial(attend, 0),
         {
-            0: [step("gather_relay", 1)],
-            1: [step("gather_last", 1), step("gather_plane", 2)],
-            3: [step("gather_relay", 2)],
+            1: [step("gather_last", 1), step("gather_relay", 2)],
+            3: [step("gather_wait", 1), step("gather_plane", 3), step("gather_start", 4), step("gather_last", 2)],
         },
+    )
+    crop_loop(functools.partial(project, 1))
+    crop_loop(
+        functools.partial(attend, 1),
+        {
+            1: [step("gather_wait", 2), step("gather_relay", 3)],
+            3: [step("gather_plane", 4), step("gather_start", 5), step("gather_last", 3)],
+        },
+    )
+    crop_loop(functools.partial(project, 2))
+    crop_loop(
+        functools.partial(attend, 2),
+        {1: [step("gather_relay", 4)], 3: [step("gather_plane", 5), step("gather_start", 6), step("gather_last", 4)]},
     )
 
     def body(c):
@@ -492,9 +529,9 @@
         root1[r, :] = jnp.broadcast_to(root, (CROP, 128))
         fl[r, :] = (n * vrow(3) + vrow(4)).astype(bf)
 
-    crop_loop(body)
-    step("gather_last", 2)()
-    step("gather_wait", 1)()
+    crop_loop(
+        body, {1: [step("gather_wait", 3)], 3: [step("gather_wait", 4), step("gather_relay", 5)]}
+    )
 
     def body(c):
         r = rows_of(c)
@@ -503,10 +540,16 @@
             u = dg(a, mat(1, j), 1, 0) + vrow(5 + j)
             g, d = gelu_parts(u)
             act[r, j * D : (j + 1) * D] = g.astype(bf)
-            gp[r, j * D : (j + 1) * D] = d.astype(bf)
-
-    crop_loop(body)
-    step("gather_wait", 2)()
+            gp[j // 2, j % 2, r, :] = d.astype(bf)
+
+    crop_loop(
+        body,
+        {
+            0: [step("gather_last", 5)],
+            1: [step("gather_plane", 6)],
+            3: [step("gather_wait", 5), step("gather_relay", 6), step("gather_last", 6), step("gather_wait", 6)],
+        },
+    )
 
     def body(c):
         r = rows_of(c)
@@ -515,7 +558,7 @@
         h = h - lane_mean(h)
         root = lax.rsqrt(lane_mean(h * h) + norm_epsilon)
         n = h * root
-        G = cot[r, :].astype(f32) * lanes(keep[r, :], 6)
+        G = cot[r, :].astype(f32) * lanes(keep[r, :].astype(f32), 6)
         cot[r, :] = (n * vrow(10) + vrow(11)).astype(bf)
         vg_ref[10:11, :] += jnp.sum(G * n, axis=0, keepdims=True)
         vg_ref[11:12, :] += jnp.sum(G, axis=0, keepdims=True)
@@ -535,8 +578,8 @@
         a = gsec[r, :]
         for j in range(4):
             ga = dg(a, mat(2, j), 1, 1)
-            gi = (ga * gp[r, j * D : (j + 1) * D].astype(f32)).astype(bf)
-            gp[r, j * D : (j + 1) * D] = gi
+            gi = (ga * gp[j // 2, j % 2, r, :].astype(f32)).astype(bf)
+            gp[j // 2, j % 2, r, :] = gi
             vg_ref[5 + j : 6 + j, :] += jnp.sum(gi.astype(f32), axis=0, keepdims=True)
 
     crop_loop(body)
@@ -547,13 +590,14 @@
         m = pl.ds(pl.multiple_of(i * D, D), D)
         wd[i] = dg(act[:, m], gsec[...], 0, 0).astype(bf).reshape(2, 2, 2, SUB, D)
 
-    step("sum_start", 2)()
+    step("sum_start", 5)()
+    step("sum_start", 6)()
 
     def body(c):
         r = rows_of(c)
         G = gs[r, :]
         for j in range(4):
-            G = G + dg(gp[r, j * D : (j + 1) * D], mat(1, j), 1, 1)
+            G = G + dg(gp[j // 2, j % 2, r, :], mat(1, j), 1, 1)
         n = nrm1[r, :]
         vg_ref[3:4, :] += jnp.sum(G * n, axis=0, keepdims=True)
         vg_ref[4:5, :] += jnp.sum(G, axis=0, keepdims=True)
@@ -564,38 +608,39 @@
         gsec[r, :] = gb
         vg_ref[2:3, :] += jnp.sum(gb.astype(f32), axis=0, keepdims=True)
 
-    crop_loop(body, {2: [step("sum_one", 2)]})
+    crop_loop(body, {1: [step("sum_one", 5), step("sum_one", 6)]})
 
     @pl.loop(0, 4)
     def _(j):
-        g = gp[:, pl.ds(pl.multiple_of(j * D, D), D)]
+        g = gp[j // 2, j % 2]
         ws[1, j // 2, j % 2] = dg(fl[...], g, 0, 0).astype(bf).reshape(4, 2, SUB, D)
 
-    step("sum_start", 1)()
+        @pl.when(j == 1)
+        def _():
+            step("sum_two", 5)()
+
+    step("sum_start", 3)()
+    step("sum_start", 4)()
 
     def body(c):
         r = rows_of(c)
         fl[r, :] = dg(gsec[r, :], mat(0, 3), 1, 1).astype(bf)
 
-    crop_loop(body)
-    step("sum_two", 2)()
-    step("sum_one", 1)()
-
-    def body(c):
+    crop_loop(body, {3: [step("sum_two", 6)]})
+
+    def attend_back(t, c):
         r = rows_of(c)
-        for p in range(6):
-            cq = slice(p * 128, (p + 1) * 128)
-            ck = slice(D + p * 128, D + (p + 1) * 128)
-            cv = slice(2 * D + p * 128, 2 * D + (p + 1) * 128)
-            q = qkv[r, cq] * jnp.asarray(0.125, bf)
-            k = qkv[r, ck]
-            v = qkv[r, cv]
-            do = fl[r, cq]
+        for p in range(2):
+            at = [slice(t * D + b * 256 + p * 128, t * D + b * 256 + (p + 1) * 128) for b in range(3)]
+            cols = slice(t * 256 + p * 128, t * 256 + (p + 1) * 128)
+            q, k, v = (qkv[r, cut] for cut in at)
+            q = q * jnp.asarray(0.125, bf)
+            do = fl[r, cols]
             dq = dk = dv = None
             for h in range(2):
                 dom = half(do, h)
                 dp = dg(v, dom, 1, 1)
-                prb = pt[c, 2 * p + h]
+                prb = pt[c, 4 * t + 2 * p + h]
                 pr = prb.astype(f32)
                 delta = jnp.sum(pr * dp, axis=0, keepdims=True)
                 ds = (pr * (dp - delta)).astype(bf)
@@ -605,68 +650,88 @@
                 dq, dk, dv = (tq, tk, tv) if dq is None else (dq + tq, dk + tk, dv + tv)
             dq = (dq * 0.125).astype(bf)
             dv = dv.astype(bf)
-            act[r, cq] = dq
-            act[r, ck] = dk.astype(bf)
-            act[r, cv] = dv
-            vg_ref[0:1, cq] += jnp.sum(dq.astype(f32), axis=0, keepdims=True)
-            vg_ref[1:2, cq] += jnp.sum(dv.astype(f32), axis=0, keepdims=True)
+            act[r, at[0]] = dq
+            act[r, at[1]] = dk.astype(bf)
+            act[r, at[2]] = dv
+            vg_ref[0:1, cols] += jnp.sum(dq.astype(f32), axis=0, keepdims=True)
+            vg_ref[1:2, cols] += jnp.sum(dv.astype(f32), axis=0, keepdims=True)
+
+    def third_grads(t):
+        g = dg(x[...], act[:, t * D : (t + 1) * D], 0, 0).astype(bf)
+        for j in range(3):
+            gp[j // 2, j % 2, 0:D, third(t)] = g[:, third(j)]
+        gp[1, 1, 0:D, third(t)] = dg(mixed[...], gsec[:, third(t)], 0, 0).astype(bf)
 
     crop_loop(
-        body,
+        functools.partial(attend_back, 0),
+        {1: [step("sum_one", 3), step("sum_one", 4)], 3: [step("sum_zed", 5), step("sum_zed", 6)]},
+    )
+    third_grads(0)
+    step("sum_start", 0)()
+    crop_loop(
+        functools.partial(attend_back, 1),
+        {1: [step("sum_two", 3), step("sum_one", 0)], 3: [step("sum_plane", 5), step("sum_two", 4)]},
+    )
+    third_grads(1)
+    step("sum_start", 1)()
+    crop_loop(
+        functools.partial(attend_back, 2),
         {
-            0: [step("sum_zed", 2)],
-            1: [step("sum_two", 1)],
-            2: [step("sum_plane", 2)],
-            3: [step("sum_zed", 1)],
+            1: [step("sum_two", 0), step("sum_one", 1), step("sum_plane", 6)],
+            3: [step("sum_zed", 3)],
         },
     )
     if linked:
-        net.sum_drain(2)
         net.vs[0] = vg_ref[...]
-    else:
-        vg_out[...] = vg_ref[...]
-        cp_g1 = pltpu.make_async_copy(ws.at[1], g1_h, sem.at[3])
-        cp_g2 = pltpu.make_async_copy(wd, g2_h, sem.at[2])
-        cp_g1.start()
-        cp_g2.start()
-        cp_g2.wait()
-
-    for j in range(4):
-        if j == 3:
-            g = dg(mixed[...], gsec[...], 0, 0)
-        else:
-            g = dg(x[...], act[:, j * D : (j + 1) * D], 0, 0)
-        wd[:, :, j // 2, j % 2] = g.astype(bf).reshape(4, 2, SUB, D)
-
-    step("sum_start", 0)()
+    third_grads(2)
+    step("sum_start", 2)()
 
     def body(c):
         r = rows_of(c)
         G = gs[r, :]
         for b in range(3):
-            G = G + dg(act[r, b * D : (b + 1) * D], mat(0, b), 1, 1)
+            for t in range(3):
+                G = G + dg(act[r, t * D + b * 256 : t * D + (b + 1) * 256], mat_third(b, t), 1, 1)
         gsec[r, :] = G.astype(bf)
 
-    crop_loop(body, {1: [step("sum_one", 0), step("sum_plane", 1)]})
+    crop_loop(
+        body,
+        {
+            0: [step("sum_zed", 4)],
+            1: [step("sum_one", 2), step("sum_two", 1), step("sum_zed", 0)],
+            2: [step("sum_plane", 3)],
+            3: [step("sum_two", 2), step("sum_zed", 1)],
+        },
+    )
     cp_tg = pltpu.make_async_copy(gsec, tg_h, sem.at[1])
     cp_tg.start()
     if linked:
-        net.sum_two(0)
-        net.sum_zed(0)
+        net.sum_plane(4)
+        net.sum_plane(0)
+        net.sum_zed(2)
+        net.sum_plane(1)
+        for g in (5, 6, 3, 4, 0, 1):
+            net.sum_wait(g)
+        net.sum_plane(2)
         net.sum_wait(2)
-        net.sum_wait(1)
-        net.sum_plane(0)
-        net.sum_wait(0)
-        cp_gt = pltpu.make_async_copy(net.gt, gt_h, sem.at[2])
-        cp_gt.start()
-        net.sum_drain(1)
-        net.sum_drain(0)
-        cp_gt.wait()
+        shares = [pltpu.make_async_copy(net.gt.at[i], t_h, sem.at[2 + i]) for i, t_h in enumerate((t0_h, t1_h, t2_h))]
+        for copy in shares:
+            copy.start()
+        for g in range(7):
+            net.sum_drain(g)
+        for copy in shares:
+            copy.wait()
     else:
-        cp_g0 = pltpu.make_async_copy(wd, g0_h, sem.at[2])
-        cp_g0.start()
-        cp_g0.wait()
-        cp_g1.wait()
+        vg_out[...] = vg_ref[...]
+        copies = [
+            pltpu.make_async_copy(gp.at[:, :, 0:D], g0_h, sem.at[2]),
+            pltpu.make_async_copy(ws.at[1], g1_h, sem.at[3]),
+            pltpu.make_async_copy(wd, g2_h, sem.at[4]),
+        ]
+        for copy in copies:
+            copy.start()
+        for copy in copies:
+            copy.wait()
     cp_y.wait()
     cp_tg.wait()
 
@@ -682,10 +747,10 @@
     shape = jax.ShapeDtypeStruct
     outs = [(shape((T, D), bf), hbm), (shape((T, D), bf), hbm)]
     if linked:
-        outs += [(shape((3, 4, SUB, D), bf), hbm)]
+        outs += [(shape((4, SUB, D), bf), hbm)] * 3
     else:
-        outs += [(shape(WD, bf), hbm), (shape(WS[1:], bf), hbm), (shape(WD, bf), hbm)]
-    outs += [(shape((16, D), f32), near)]
+        outs += [(shape((2, 2, D, D), bf), hbm), (shape(WS[1:], bf), hbm), (shape(WD, bf), hbm)]
+    outs += [(shape((16, 128 if linked else D), f32), near)]
     scratch = [
         VM(WS, bf),
         VM(WD, bf),
@@ -697,21 +762,24 @@
         VM((T, 128), f32),
         VM((T, D), bf),
         VM((T, FF), bf),
-        VM((T, FF), bf),
+        VM((2, 2, T, D), bf),
         VM((T, D), f32),
         VM((T, D), bf),
         VM((T, D), bf),
-        VM((T, 128), f32),
+        VM((T, 128), bf),
         VM((16, D), f32),
         VM((16, D), f32),
         pltpu.SemaphoreType.DMA((11,)),
     ]
     params = dict(vmem_limit_bytes=63 * 2**20)
     if linked:
-        transfers = 3 * (4 + 3 + 3 + 3 + 3 + 12) + 7 + 3 * (4 + 4 + 4 + 3 + 3) + 6
+        transfers = 7 * (4 + 3 + 3 + 3 + 3 + 12) + 7 + 7 * (4 + 4 + 4 + 3 + 3) + 6
         scratch += [
             VM((8, 16, 128), bf),
             VM((4, 2, 2, SUB, D), bf),
+            VM((4, 2, SUB, D), bf),
+            VM((4, SUB, D), bf),
+            VM((3, SUB, D), bf),
             VM((4, 2, SUB, D), bf),
             VM((4, SUB, D), bf),
             VM((3, SUB, D), bf),
@@ -720,13 +788,13 @@
             VM((6, 16, D), f32),
             pltpu.SemaphoreType.DMA((transfers,)),
             pltpu.SemaphoreType.DMA((transfers,)),
-            pltpu.SemaphoreType.REGULAR((8,)),
+            pltpu.SemaphoreType.REGULAR((16,)),
         ]
         params.update(collective_id=0, has_side_effects=True)
     return pl.pallas_call(
         functools.partial(layer_kernel, linked),
         out_shape=[o[0] for o in outs],
-        in_specs=[hbm, hbm, near, near] + [hbm] * (len(arrays) - 4),
+        in_specs=[hbm, hbm, near, pl.BlockSpec(memory_space=pltpu.SMEM), near] + [hbm] * (len(arrays) - 5),
         out_specs=[o[1] for o in outs],
         scratch_shapes=scratch,
         compiler_params=pltpu.CompilerParams(**params),
@@ -738,12 +806,6 @@
     second_new = decay_second * second_moment + (1.0 - decay_second) * gradient * gradient
     step_dir = first_new / correct_first / (jnp.sqrt(second_new / correct_second) + adam_epsilon)
     return (step_dir, first_new)
-
-
-def allowed_rows(deletion, lengths):
-    places = jnp.arange(CROP, dtype=jnp.int32)[None, :]
-    allowed = ((deletion == 1) | (places == 0)) & (places < lengths[:, None])
-    return jnp.pad(allowed.astype(f32), ((0, 8 - NC), (0, 0)))
 
 
 def finish(output, token_grad, gradients, moments):
@@ -760,22 +822,78 @@
     return jnp.concatenate([blocks[j] for j in range(blocks.shape[0])], axis=1)
 
 
+def adam_kernel(*refs):
+    sums, moments, passed, outs, placed = refs[:4], refs[4:14], refs[14:16], refs[16:31], refs[31:33]
+    hold, sem = refs[33:]
+    fetch = [pltpu.make_async_copy(a, hold.at[i], sem.at[i]) for i, a in enumerate(passed)]
+    store = [pltpu.make_async_copy(hold.at[i], a, sem.at[2 + i]) for i, a in enumerate(placed)]
+
+    @pl.when(pl.program_id(0) == 0)
+    def _():
+        for copy in fetch:
+            copy.start()
+
+    @pl.when(pl.program_id(0) == 1)
+    def _():
+        for i in range(2):
+            fetch[i].wait()
+            store[i].start()
+
+    square, up, down, vec = (ref[...] for ref in sums)
+
+    def update(k, cut, g):
+        at = Ellipsis if cut is None else (slice(None), cut)
+        g = g.astype(f32)
+        step, first = adam_update(g, moments[k][at], moments[5 + k][at])
+        outs[k][at] = g
+        outs[5 + k][at] = step
+        outs[10 + k][at] = first
+
+    for j in range(4):
+        cut = slice(j * D, (j + 1) * D)
+        update(*((0, cut) if j < 3 else (1, None)), square[j])
+        update(2, cut, up[j])
+    update(3, None, down)
+
+    @pl.when(pl.program_id(0) == 0)
+    def _():
+        rows, width = outs[4].shape
+        update(4, None, vec[0:rows, 0:width])
+
+    @pl.when(pl.program_id(0) == pl.num_programs(0) - 1)
+    def _():
+        for copy in store:
+            copy.wait()
+
+
+def adam(sums, moments, passed, steps=3):
+    def rows(shape):
+        return pl.BlockSpec((shape[0] // steps, shape[1]), lambda i: (i, 0))
+
+    def whole(shape):
+        return pl.BlockSpec(shape, lambda i: (0, 0))
+
+    hbm = pl.BlockSpec(memory_space=pl.ANY)
+    parts = pl.BlockSpec((4, SUB // steps, D), lambda i: (0, i, 0))
+    specs = [whole(m.shape) if k == 4 else rows(m.shape) for k, m in enumerate(moments[:5])]
+    return pl.pallas_call(
+        adam_kernel,
+        grid=(steps,),
+        out_shape=[jax.ShapeDtypeStruct(m.shape, f32) for m in moments[:5]] * 3
+        + [jax.ShapeDtypeStruct(a.shape, a.dtype) for a in passed],
+        in_specs=[parts, parts, rows((4 * SUB, D)), whole((16, 128))] + specs * 2 + [hbm] * 2,
+        out_specs=specs * 3 + [hbm] * 2,
+        scratch_shapes=[pltpu.VMEM((2, *passed[0].shape), bf), pltpu.SemaphoreType.DMA((4,))],
+        compiler_params=pltpu.CompilerParams(vmem_limit_bytes=63 * 2**20),
+    )(*sums, *moments, *passed)
+
+
 def per_device_linked(tokens, cotangent, deletion, lengths, qkv, out, up, down, vectors, *moments):
-    vec = jnp.pad(vectors.astype(bf), ((0, 4), (0, 128 - vectors.shape[1])))
-    output, token_grad, sums, vector_sums = layer(
-        True, tokens, cotangent, allowed_rows(deletion, lengths), vec, qkv, out, up, down
-    )
-    sums = sums.astype(f32)
-    width = vectors.shape[1]
-    vec = lax.dynamic_slice(vector_sums, (0, lax.axis_index("shard") * width), (12, width))
-    gradients = (
-        side_by_side(sums[0, :3]),
-        sums[0, 3],
-        side_by_side(sums[1]),
-        sums[2].reshape(4 * SUB, D),
-        vec,
-    )
-    return finish(output, token_grad, gradients, moments)
+    output, token_grad, square, tall, wide, vec = layer(
+        True, tokens, cotangent, deletion, lengths, vectors, qkv, out, up, down
+    )
+    *updated, output, token_grad = adam((square, tall, wide.reshape(4 * SUB, D), vec), moments, (output, token_grad))
+    return (output, token_grad) + tuple(updated)
 
 
 def per_device_plain(tokens, cotangent, deletion, lengths, qkv, out, up, down, vectors, *moments):
@@ -788,12 +906,13 @@
         False,
         tokens,
         cotangent,
-        allowed_rows(deletion, lengths),
+        deletion,
+        lengths,
         jnp.pad(vec, ((0, 4), (0, 0))),
         square.reshape(WS),
         tall.reshape(WD),
     )
-    g0 = g0.transpose(2, 3, 0, 1, 4, 5).reshape(4, D, D)
+    g0 = g0.reshape(4, D, D)
     square = lax.psum_scatter(
         jnp.concatenate([g0, g1.reshape(4, D, D)]).astype(f32), "shard", scatter_dimension=1, tiled=True
     )

time: 240 us -> 193 us (0.80)
  the two profiles are of different devices: /device:TPU:28 before, /device:TPU:0 now
where the time goes in v3:
time: 193 us
  Pallas kernels  192 us (99%)
    pallas_call x1, Pallas kernels, layer(): pl.pallas_call(functools.partial(layer_kernel, linked), out_shape=[o[0] f...  182 us
    pallas_call x1, Pallas kernels, adam(): pl.pallas_call(adam_kernel, grid=(steps,), out_shape=[jax.ShapeDtypeStruc...  9.98 us

profile of v3, /device:TPU:0, one launch (start us, length us, event | category | flops | bytes accessed | tf_op | source)
XLA Modules:
  0.0 193.2 jit_solution(406937021728215683)
XLA Ops:
  0.7 182.3 %shard_map.314 = (bf16[1024,768]{1,0:T(8,128)(2,1)}, bf16[1024,768]{1,0:T(8,128)(2,1)}, bf16[4,96,768]{2,1,0:T(8,128)(2,1)}, bf16[4,96,768]{2,1,0:T(8,128)(2,1)}...) custom-call(bf16[1024,768]{1,0:T(8,128)(2,1)} %refs_0_.1, bf16[1024,768]{1,0:T(8,128)(2,1)} %refs_1_.1, ...), custom_call_target="tpu_custom_call" | custom-call | tf_op jit(solution)/shard_map/pallas_call | solution.py:794
  183.0 10.0 %shard_map.315 = (f32[96,2304]{1,0:T(8,128)}, f32[96,768]{1,0:T(8,128)}, f32[96,3072]{1,0:T(8,128)}, f32[384,768]{1,0:T(8,128)}, f32[12,96]{1,0:T(8,128)}, /*ind...) custom-call(bf16[4,96,768]{2,1,0:T(8,128)(2,1)} %get-tuple-element.4, ...), custom_call_target="tpu_custom_call" | custom-call | tf_op jit(solution)/shard_map/pallas_call | solution.py:879

commit v4 on v3

--- a/solution.py
+++ b/solution.py
@@ -18,6 +18,81 @@
 bf = jnp.bfloat16
 f32 = jnp.float32
 MESH = pl.DeviceIdType.MESH
+Z_FIRST = (4, 6, 2)
+GATHER_PLAN = {
+    "start": {
+        0: [("start", 1), ("plane", 0), ("start", 2), ("plane", 1), ("relay", 0), ("start", 3), ("plane", 2), ("relay", 1), ("last", 0), ("wait", 0)],
+    },
+    "project0": {
+        1: [("start", 4), ("relay", 2)],
+        2: [("plane", 3), ("last", 1)],
+    },
+    "attend0": {
+        0: [("wait", 1), ("last", 2)],
+        2: [("wait", 2), ("start", 5)],
+        3: [("plane", 4), ("relay", 3)],
+    },
+    "attend1": {
+        2: [("start", 6)],
+        3: [("relay", 4), ("plane", 5)],
+    },
+    "project2": {
+        1: [("last", 3)],
+    },
+    "attend2": {
+        0: [("wait", 3), ("last", 4)],
+        2: [("wait", 4), ("plane", 6)],
+        3: [("relay", 5)],
+    },
+    "up": {
+        0: [("relay", 6)],
+        1: [("last", 5)],
+        2: [("last", 6), ("wait", 5)],
+        3: [("wait", 6)],
+    },
+}
+SUM_PLAN = {
+    "down_grad": {
+        0: [("start", 5), ("start", 6)],
+    },
+    "first_back": {
+        1: [("one", 5)],
+        2: [("half", 6)],
+    },
+    "up_grad": {
+        2: [("two", 5)],
+        3: [("start", 3), ("start", 4)],
+    },
+    "attend_back0": {
+        0: [("zed", 5), ("one", 3)],
+        1: [("one", 6), ("half", 4)],
+    },
+    "grads0": {
+        0: [("start", 0), ("plane", 5)],
+    },
+    "attend_back1": {
+        0: [("two", 3)],
+        1: [("one", 0), ("two", 6)],
+    },
+    "grads1": {
+        0: [("wait", 5), ("start", 1)],
+    },
+    "attend_back2": {
+        0: [("zed", 3)],
+        1: [("one", 4), ("one", 1)],
+        2: [("two", 0)],
+        3: [("zed", 6)],
+    },
+    "grads2": {
+        0: [("plane", 3), ("start", 2), ("two", 4)],
+    },
+    "token": {
+        1: [("plane", 6), ("half", 2), ("two", 1)],
+    },
+    "end": {
+        0: [("zed", 0), ("wait", 3), ("zed", 4), ("one", 2), ("wait", 6), ("zed", 1), ("plane", 0), ("two", 2), ("plane", 4), ("wait", 0), ("zed", 2), ("plane", 1), ("wait", 4), ("plane", 2), ("wait", 1), ("wait", 2)],
+    },
+}
 
 norm_epsilon = 1e-06
 decay_first = 0.9
@@ -57,11 +132,11 @@
     return u * cdf, cdf + u * density
 
 
-def crop_loop(body, after=None):
+def crop_loop(body, after):
     @pl.loop(0, NC)
     def _(c):
         body(c)
-        for k, steps in (after or {}).items():
+        for k, steps in after.items():
 
             @pl.when(c == k)
             def _():
@@ -90,6 +165,10 @@
         self.s1 = self.z * 2 + self.c1
         self.s_others = [z * 2 + self.c for z in self.others]
         self.s1_others = [z * 2 + self.c1 for z in self.others]
+        z1 = self.z // 2 * 2 + 1 - self.z % 2
+        self.dev_z1 = (r, z1 * 2 + self.c)
+        self.z_give = [1 - self.z % 2, 3 - self.z % 2]
+        self.z_keep = [self.z % 2, 2 + self.z % 2]
         self.count = 0
         self.sent = []
 
@@ -121,15 +200,17 @@
             return self.wd.at[z, c, jy, jx, :, columns(g)]
         return self.ws.at[g // 3, jy, jx, z, c, :, columns(g)]
 
+    def column(self, g, jy, jx, c):
+        return self.part(g, jy, jx, slice(None), c)
+
     def plan_gather(self):
         self.ag = [
             dict(
-                core=[self.slot() for _ in range(4)],
                 zed=[self.slot() for _ in range(3)],
                 px=[self.slot() for _ in range(3)],
                 py=[self.slot() for _ in range(3)],
                 relay=[self.slot() for _ in range(3)],
-                sib=[[self.slot() for _ in range(3)] for _ in range(4)],
+                sib=[self.slot() for _ in range(4)],
             )
             for _ in range(7)
         ]
@@ -154,10 +235,6 @@
         self.copy(ref[0](*ref[1:]), ref[0](*ref[1:]), k, device).wait_recv()
 
     def gather_start(self, g):
-        for j in range(4):
-            self.same(
-                (self.part, g, j // 2, j % 2, self.z, self.c), self.ag[g]["core"][j], self.dev_core, self.sent
-            )
         own = (self.part, g, self.y, self.x, self.z, self.c)
         for d in range(3):
             self.same(own, self.ag[g]["zed"][d], self.dev_z[d], self.sent)
@@ -177,11 +254,12 @@
             self.arrive(ref, self.ag[g]["zed"][k], self.dev_z[d])
             self.same(ref, self.ag[g]["px"][d], self.dev_x, self.sent)
             self.same(ref, self.ag[g]["py"][d], self.dev_y, self.sent)
-            self.same(ref, self.ag[g]["sib"][0][d], self.dev_core, self.sent)
             if g == 0:
                 block = (self.at, "vb", self.s_others[d])
                 self.arrive(block, self.ag_vec["zed"][k], self.dev_z[d])
                 self.same(block, self.ag_vec["sib"][d], self.dev_core, self.sent)
+
+        self.same((self.column, g, self.y, self.x, self.c), self.ag[g]["sib"][0], self.dev_core, self.sent)
 
     def gather_relay(self, g):
         for d in range(3):
@@ -190,23 +268,23 @@
             self.arrive(ref_x, self.ag[g]["px"][d], self.dev_x)
             if self.x_first(g, d):
                 self.same(ref_x, self.ag[g]["relay"][d], self.dev_y, self.sent)
-            self.same(ref_x, self.ag[g]["sib"][1][d], self.dev_core, self.sent)
             ref_y = (self.part, g, self.y1, self.x, z, self.c)
             self.arrive(ref_y, self.ag[g]["py"][d], self.dev_y)
             if not self.x_first(g, d):
                 self.same(ref_y, self.ag[g]["relay"][d], self.dev_x, self.sent)
-            self.same(ref_y, self.ag[g]["sib"][2][d], self.dev_core, self.sent)
+
+        self.same((self.column, g, self.y, self.x1, self.c), self.ag[g]["sib"][1], self.dev_core, self.sent)
+        self.same((self.column, g, self.y1, self.x, self.c), self.ag[g]["sib"][2], self.dev_core, self.sent)
 
     def gather_last(self, g):
         for d in range(3):
             ref = (self.part, g, self.y1, self.x1, self.others[d], self.c)
             self.arrive(ref, self.ag[g]["relay"][d], self.dev_y if self.x_first(g, d) else self.dev_x)
-            self.same(ref, self.ag[g]["sib"][3][d], self.dev_core, self.sent)
+
+        self.same((self.column, g, self.y1, self.x1, self.c), self.ag[g]["sib"][3], self.dev_core, self.sent)
 
     def gather_wait(self, g):
         c = self.c1
-        for j in range(4):
-            self.arrive((self.part, g, j // 2, j % 2, self.z, c), self.ag[g]["core"][j], self.dev_core)
         spots = [
             (self.y, self.x),
             (self.y, self.x1),
@@ -214,8 +292,7 @@
             (self.y1, self.x1),
         ]
         for j, (jy, jx) in enumerate(spots):
-            for d in range(3):
-                self.arrive((self.part, g, jy, jx, self.others[d], c), self.ag[g]["sib"][j][d], self.dev_core)
+            self.arrive((self.column, g, jy, jx, c), self.ag[g]["sib"][j], self.dev_core)
         if g == 0:
             self.arrive((self.at, "vb", self.s1), self.ag_vec["core"], self.dev_core)
             for d in range(3):
@@ -232,6 +309,7 @@
                 core=[self.slot() for _ in range(4)],
                 one=[self.slot() for _ in range(4)],
                 two=[self.slot() for _ in range(4)],
+                half=[self.slot() for _ in range(2)],
                 zed=[self.slot() for _ in range(3)],
                 plane=[self.slot() for _ in range(3)],
             )
@@ -251,6 +329,10 @@
         ref = getattr(self, name if name == "rc" or g > 2 else name + "t")
         return ref.at[index + (slice(None),) * (len(ref.shape) - len(index) - 1) + (columns(g),)]
 
+    def halved(self, g, k):
+        cols = slice(0, 384) if g == 4 else slice(384, 768 if g > 2 else 640)
+        return self.act3.at[k, :, :, 0:SUB, cols]
+
     def total(self, g, r):
         return self.gt.at[0 if g < 3 else (g - 1) // 2, r, :, columns(g)]
 
@@ -260,12 +342,12 @@
 
     def spend(self, g, i):
         for h in range(2):
-            if g == 3 + h or (g == 0 and i == 0):
+            if g == 3 + h or (g == h and i == 0):
                 pl.semaphore_wait(self.credit_sem.at[h * 8 + i], 1)
 
     def add(self, ref, other):
         ref, other = ref[0](*ref[1:]), other[0](*other[1:])
-        ref[...] = (ref[...].astype(f32) + other[...].astype(f32)).astype(bf)
+        ref[...] = ref[...] + other[...]
 
     def sum_start(self, g):
         self.spend(g, 0)
@@ -276,20 +358,44 @@
         if g == 2:
             self.send((self.at, "vs", 0), (self.at, "vr", 0), self.rs_vec["core"], self.dev_core, self.out[g])
 
+    def items(self, g):
+        if g in Z_FIRST:
+            return [(0, self.z_keep[0]), (2, self.z_keep[1])]
+        return [(z, z) for z in range(4)]
+
+    def sum_half(self, g):
+        c = self.c
+        for z in range(4):
+            self.arrive((self.land, "rc", g, z), self.rs[g]["core"][z], self.dev_core)
+            self.add((self.grads, g, z, c), (self.land, "rc", g, z))
+        self.credit(g, 0, self.dev_core)
+        pl.semaphore_signal(self.half_sem.at[g], inc=1, device_id=self.dev_z1, device_id_type=MESH)
+        pl.semaphore_wait(self.half_sem.at[g], 1)
+        for k in range(2):
+            self.send(
+                (self.grads, g, self.z_give[k], c), (self.halved, g, k), self.rs[g]["half"][k], self.dev_z1, self.out[g]
+            )
+
     def sum_one(self, g):
         y, x, c = self.y, self.x, self.c
-        for z in range(4):
-            mine, came = (self.grads, g, z, c), (self.land, "rc", g, z)
-            self.arrive(came, self.rs[g]["core"][z], self.dev_core)
+        for i, (slot, z) in enumerate(self.items(g)):
+            mine, came = (self.grads, g, z, c), (self.land, "rc", g, i)
+            if g in Z_FIRST:
+                came = (self.halved, g, i)
+                self.arrive(came, self.rs[g]["half"][i], self.dev_z1)
+            else:
+                self.arrive(came, self.rs[g]["core"][i], self.dev_core)
             self.add(mine, came)
-            if z == 0:
+            if i == 0:
                 self.spend(g, 1)
                 self.spend(g, 2)
-            if z < 2:
-                self.send((self.grads, g, z, c, slice(None), self.x1), (self.land, "r1", g, z), self.rs[g]["one"][z], self.dev_x, self.out[g])
+            land = (self.land, "r1", g, slot)
+            if slot < 2:
+                self.send((self.grads, g, z, c, slice(None), self.x1), land, self.rs[g]["one"][i], self.dev_x, self.out[g])
             else:
-                self.send((self.grads, g, z, c, self.y1), (self.land, "r1", g, z), self.rs[g]["one"][z], self.dev_y, self.out[g])
-        self.credit(g, 0, self.dev_core)
+                self.send((self.grads, g, z, c, self.y1), land, self.rs[g]["one"][i], self.dev_y, self.out[g])
+        if g not in Z_FIRST:
+            self.credit(g, 0, self.dev_core)
         if g == 2:
             self.arrive((self.at, "vr", 0), self.rs_vec["core"], self.dev_core)
             self.vs[1] = self.vs[0] + self.vr[0]
@@ -297,17 +403,18 @@
 
     def sum_two(self, g):
         y, x, c = self.y, self.x, self.c
-        for z in range(4):
-            came = (self.land, "r1", g, z)
-            self.arrive(came, self.rs[g]["one"][z], self.dev_x if z < 2 else self.dev_y)
-            self.add((self.grads, g, z, c, slice(None), x) if z < 2 else (self.grads, g, z, c, y), came)
-            if z == 0:
+        for i, (slot, z) in enumerate(self.items(g)):
+            came = (self.land, "r1", g, slot)
+            self.arrive(came, self.rs[g]["one"][i], self.dev_x if slot < 2 else self.dev_y)
+            self.add((self.grads, g, z, c, slice(None), x) if slot < 2 else (self.grads, g, z, c, y), came)
+            if i == 0:
                 self.spend(g, 3)
                 self.spend(g, 4)
-            if z < 2:
-                self.send((self.grads, g, z, c, self.y1, x), (self.land, "r2", g, z), self.rs[g]["two"][z], self.dev_y, self.out[g])
+            land = (self.land, "r2", g, slot)
+            if slot < 2:
+                self.send((self.grads, g, z, c, self.y1, x), land, self.rs[g]["two"][i], self.dev_y, self.out[g])
             else:
-                self.send((self.grads, g, z, c, y, self.x1), (self.land, "r2", g, z), self.rs[g]["two"][z], self.dev_x, self.out[g])
+                self.send((self.grads, g, z, c, y, self.x1), land, self.rs[g]["two"][i], self.dev_x, self.out[g])
         self.credit(g, 1, self.dev_x)
         self.credit(g, 2, self.dev_y)
         if g == 2:
@@ -317,19 +424,29 @@
 
     def sum_zed(self, g):
         y, x, c = self.y, self.x, self.c
-        for z in range(4):
-            came = (self.land, "r2", g, z)
-            self.arrive(came, self.rs[g]["two"][z], self.dev_y if z < 2 else self.dev_x)
+        for i, (slot, z) in enumerate(self.items(g)):
+            came = (self.land, "r2", g, slot)
+            self.arrive(came, self.rs[g]["two"][i], self.dev_y if slot < 2 else self.dev_x)
             self.add((self.grads, g, z, c, y, x), came)
         for d in range(3):
             self.spend(g, 5 + d)
+        if g in Z_FIRST:
             self.send(
-                (self.grads, g, self.others[d], c, y, x),
-                (self.land, "rz", g, 2 - d),
-                self.rs[g]["zed"][d],
-                self.dev_z[d],
+                (self.grads, g, self.others[1], c, y, x),
+                (self.land, "rz", g, 1),
+                self.rs[g]["zed"][1],
+                self.dev_z[1],
                 self.out[g],
             )
+        else:
+            for d in range(3):
+                self.send(
+                    (self.grads, g, self.others[d], c, y, x),
+                    (self.land, "rz", g, 2 - d),
+                    self.rs[g]["zed"][d],
+                    self.dev_z[d],
+                    self.out[g],
+                )
         self.credit(g, 3, self.dev_y)
         self.credit(g, 4, self.dev_x)
         if g == 2:
@@ -340,7 +457,7 @@
 
     def sum_plane(self, g):
         total = self.grads(g, self.z, self.c, self.y, self.x)[...].astype(f32)
-        for d in range(3):
+        for d in (1,) if g in Z_FIRST else range(3):
             self.arrive((self.land, "rz", g, d), self.rs[g]["zed"][2 - d], self.dev_z[d])
             total = total + self.land("rz", g, d)[...].astype(f32)
         own = (self.total, g, self.r)
@@ -375,10 +492,10 @@
         (tok_h, cot_h, del_ref, len_ref, vec_in, ws_h, wd_h) = refs[:7]
         (y_h, tg_h, g0_h, g1_h, g2_h, vg_out) = refs[7:13]
         rest = refs[13:]
-    (ws, wd, x, qkv, pt, mixed, nrm1, root1, fl, act, gp, gs, gsec, cot, keep, vec_ref, vg_ref, sem) = rest[:18]
+    (ws, wd, x, qkv, pt, mixed, nrm1, root1, fl, act, act3, gp, gs, gsec, cot, keep, vec_ref, vg_ref, sem) = rest[:19]
     if linked:
-        names = ("vb", "rc", "r1", "r2", "rz", "r1t", "r2t", "rzt", "gt", "vs", "vr", "send_sem", "recv_sem", "credit_sem")
-        net = Links(dict(zip(names, rest[18:]), ws=ws, wd=wd, gp=gp, vec_total=vg_out))
+        names = ("vb", "rc", "r1", "r2", "rz", "r1t", "r2t", "rzt", "gt", "vs", "vr", "send_sem", "recv_sem", "credit_sem", "half_sem")
+        net = Links(dict(zip(names, rest[19:]), ws=ws, wd=wd, gp=gp, act3=act3, vec_total=vg_out))
         net.plan_gather()
         net.plan_sum()
 
@@ -403,6 +520,17 @@
 
     def step(name, *a):
         return functools.partial(getattr(net, name), *a) if linked else (lambda: None)
+
+    def after(name):
+        plan = {}
+        for kind, table in (("gather_", GATHER_PLAN), ("sum_", SUM_PLAN)):
+            for c, steps in table.get(name, {}).items():
+                plan[c] = [step(kind + what, g) for what, g in steps]
+        return plan
+
+    def now(name):
+        for act_now in after(name).get(0, ()):
+            act_now()
 
     if linked:
         net.greet()
@@ -454,13 +582,7 @@
     cp_x.wait()
     cp_cot.wait()
     if linked:
-        net.gather_plane(0)
-        net.gather_start(1)
-        net.gather_relay(0)
-        net.gather_plane(1)
-        net.gather_start(2)
-        net.gather_last(0)
-        net.gather_wait(0)
+        now("start")
         row = lax.broadcasted_iota(jnp.int32, (128, D), 0)
         col = lax.broadcasted_iota(jnp.int32, (128, D), 1)
         vec = jnp.zeros((16, D), f32)
@@ -497,27 +619,9 @@
                 o = w if o is None else o + w
             mixed[r, t * 256 + p * 128 : t * 256 + (p + 1) * 128] = o.astype(bf)
 
-    crop_loop(functools.partial(project, 0), {0: [step("gather_relay", 1), step("gather_plane", 2), step("gather_start", 3)]})
-    crop_loop(
-        functools.partial(attend, 0),
-        {
-            1: [step("gather_last", 1), step("gather_relay", 2)],
-            3: [step("gather_wait", 1), step("gather_plane", 3), step("gather_start", 4), step("gather_last", 2)],
-        },
-    )
-    crop_loop(functools.partial(project, 1))
-    crop_loop(
-        functools.partial(attend, 1),
-        {
-            1: [step("gather_wait", 2), step("gather_relay", 3)],
-            3: [step("gather_plane", 4), step("gather_start", 5), step("gather_last", 3)],
-        },
-    )
-    crop_loop(functools.partial(project, 2))
-    crop_loop(
-        functools.partial(attend, 2),
-        {1: [step("gather_relay", 4)], 3: [step("gather_plane", 5), step("gather_start", 6), step("gather_last", 4)]},
-    )
+    for t in range(3):
+        crop_loop(functools.partial(project, t), after(f"project{t}"))
+        crop_loop(functools.partial(attend, t), after(f"attend{t}"))
 
     def body(c):
         r = rows_of(c)
@@ -529,9 +633,7 @@
         root1[r, :] = jnp.broadcast_to(root, (CROP, 128))
         fl[r, :] = (n * vrow(3) + vrow(4)).astype(bf)
 
-    crop_loop(
-        body, {1: [step("gather_wait", 3)], 3: [step("gather_wait", 4), step("gather_relay", 5)]}
-    )
+    crop_loop(body, after("out"))
 
     def body(c):
         r = rows_of(c)
@@ -539,21 +641,18 @@
         for j in range(4):
             u = dg(a, mat(1, j), 1, 0) + vrow(5 + j)
             g, d = gelu_parts(u)
-            act[r, j * D : (j + 1) * D] = g.astype(bf)
+            if j < 3:
+                act[r, j * D : (j + 1) * D] = g.astype(bf)
+            else:
+                act3[c // 2, c % 2] = g.astype(bf).reshape(2, 128, D)
             gp[j // 2, j % 2, r, :] = d.astype(bf)
 
-    crop_loop(
-        body,
-        {
-            0: [step("gather_last", 5)],
-            1: [step("gather_plane", 6)],
-            3: [step("gather_wait", 5), step("gather_relay", 6), step("gather_last", 6), step("gather_wait", 6)],
-        },
-    )
+    crop_loop(body, after("up"))
 
     def body(c):
         r = rows_of(c)
-        s = dg(act[r, :], wd[...].reshape(FF, D), 1, 0) + vrow(9)
+        s = dg(act[r, :], wd[0:3].reshape(3 * D, D), 1, 0)
+        s = s + dg(act3[c // 2, c % 2].reshape(CROP, D), wd[3].reshape(D, D), 1, 0) + vrow(9)
         h = nrm1[r, :] * vrow(3) + vrow(4) + s
         h = h - lane_mean(h)
         root = lax.rsqrt(lane_mean(h * h) + norm_epsilon)
@@ -569,7 +668,7 @@
         gsec[r, :] = gb
         vg_ref[9:10, :] += jnp.sum(gb.astype(f32), axis=0, keepdims=True)
 
-    crop_loop(body)
+    crop_loop(body, after("down"))
     cp_y = pltpu.make_async_copy(cot, y_h, sem.at[0])
     cp_y.start()
 
@@ -582,16 +681,17 @@
             gp[j // 2, j % 2, r, :] = gi
             vg_ref[5 + j : 6 + j, :] += jnp.sum(gi.astype(f32), axis=0, keepdims=True)
 
-    crop_loop(body)
+    crop_loop(body, after("act_back"))
     step("gather_drain")()
 
-    @pl.loop(0, 4)
+    @pl.loop(0, 3)
     def _(i):
         m = pl.ds(pl.multiple_of(i * D, D), D)
         wd[i] = dg(act[:, m], gsec[...], 0, 0).astype(bf).reshape(2, 2, 2, SUB, D)
 
-    step("sum_start", 5)()
-    step("sum_start", 6)()
+    wd[3] = dg(act3[...].reshape(T, D), gsec[...], 0, 0).astype(bf).reshape(2, 2, 2, SUB, D)
+
+    now("down_grad")
 
     def body(c):
         r = rows_of(c)
@@ -608,25 +708,18 @@
         gsec[r, :] = gb
         vg_ref[2:3, :] += jnp.sum(gb.astype(f32), axis=0, keepdims=True)
 
-    crop_loop(body, {1: [step("sum_one", 5), step("sum_one", 6)]})
-
-    @pl.loop(0, 4)
-    def _(j):
-        g = gp[j // 2, j % 2]
-        ws[1, j // 2, j % 2] = dg(fl[...], g, 0, 0).astype(bf).reshape(4, 2, SUB, D)
-
-        @pl.when(j == 1)
-        def _():
-            step("sum_two", 5)()
-
-    step("sum_start", 3)()
-    step("sum_start", 4)()
+    crop_loop(body, after("first_back"))
+
+    def body(j):
+        ws[1, j // 2, j % 2] = dg(fl[...], gp[j // 2, j % 2], 0, 0).astype(bf).reshape(4, 2, SUB, D)
+
+    crop_loop(body, after("up_grad"))
 
     def body(c):
         r = rows_of(c)
         fl[r, :] = dg(gsec[r, :], mat(0, 3), 1, 1).astype(bf)
 
-    crop_loop(body, {3: [step("sum_two", 6)]})
+    crop_loop(body, after("mixed_back"))
 
     def attend_back(t, c):
         r = rows_of(c)
@@ -662,29 +755,12 @@
             gp[j // 2, j % 2, 0:D, third(t)] = g[:, third(j)]
         gp[1, 1, 0:D, third(t)] = dg(mixed[...], gsec[:, third(t)], 0, 0).astype(bf)
 
-    crop_loop(
-        functools.partial(attend_back, 0),
-        {1: [step("sum_one", 3), step("sum_one", 4)], 3: [step("sum_zed", 5), step("sum_zed", 6)]},
-    )
-    third_grads(0)
-    step("sum_start", 0)()
-    crop_loop(
-        functools.partial(attend_back, 1),
-        {1: [step("sum_two", 3), step("sum_one", 0)], 3: [step("sum_plane", 5), step("sum_two", 4)]},
-    )
-    third_grads(1)
-    step("sum_start", 1)()
-    crop_loop(
-        functools.partial(attend_back, 2),
-        {
-            1: [step("sum_two", 0), step("sum_one", 1), step("sum_plane", 6)],
-            3: [step("sum_zed", 3)],
-        },
-    )
-    if linked:
-        net.vs[0] = vg_ref[...]
-    third_grads(2)
-    step("sum_start", 2)()
+    for t in range(3):
+        crop_loop(functools.partial(attend_back, t), after(f"attend_back{t}"))
+        if linked and t == 2:
+            net.vs[0] = vg_ref[...]
+        third_grads(t)
+        now(f"grads{t}")
 
     def body(c):
         r = rows_of(c)
@@ -694,26 +770,11 @@
                 G = G + dg(act[r, t * D + b * 256 : t * D + (b + 1) * 256], mat_third(b, t), 1, 1)
         gsec[r, :] = G.astype(bf)
 
-    crop_loop(
-        body,
-        {
-            0: [step("sum_zed", 4)],
-            1: [step("sum_one", 2), step("sum_two", 1), step("sum_zed", 0)],
-            2: [step("sum_plane", 3)],
-            3: [step("sum_two", 2), step("sum_zed", 1)],
-        },
-    )
+    crop_loop(body, after("token"))
     cp_tg = pltpu.make_async_copy(gsec, tg_h, sem.at[1])
     cp_tg.start()
     if linked:
-        net.sum_plane(4)
-        net.sum_plane(0)
-        net.sum_zed(2)
-        net.sum_plane(1)
-        for g in (5, 6, 3, 4, 0, 1):
-            net.sum_wait(g)
-        net.sum_plane(2)
-        net.sum_wait(2)
+        now("end")
         shares = [pltpu.make_async_copy(net.gt.at[i], t_h, sem.at[2 + i]) for i, t_h in enumerate((t0_h, t1_h, t2_h))]
         for copy in shares:
             copy.start()
@@ -761,7 +822,8 @@
         VM((T, D), f32),
         VM((T, 128), f32),
         VM((T, D), bf),
-        VM((T, FF), bf),
+        VM((T, 3 * D), bf),
+        VM((2, 2, 2, 128, D), bf),
         VM((2, 2, T, D), bf),
         VM((T, D), f32),
         VM((T, D), bf),
@@ -773,7 +835,7 @@
     ]
     params = dict(vmem_limit_bytes=63 * 2**20)
     if linked:
-        transfers = 7 * (4 + 3 + 3 + 3 + 3 + 12) + 7 + 7 * (4 + 4 + 4 + 3 + 3) + 6
+        transfers = 7 * (3 + 3 + 3 + 3 + 4) + 7 + 7 * (4 + 4 + 4 + 2 + 3 + 3) + 6
         scratch += [
             VM((8, 16, 128), bf),
             VM((4, 2, 2, SUB, D), bf),
@@ -789,6 +851,7 @@
             pltpu.SemaphoreType.DMA((transfers,)),
             pltpu.SemaphoreType.DMA((transfers,)),
             pltpu.SemaphoreType.REGULAR((16,)),
+            pltpu.SemaphoreType.REGULAR((7,)),
         ]
         params.update(collective_id=0, has_side_effects=True)
     return pl.pallas_call(

time: 193 us -> 189 us (0.979)
  Pallas kernels: 192 us -> 188 us
    pallas_call x1, Pallas kernels: 182 us -> 178 us  [layer(): pl.pallas_call(functools.partial(layer_kernel, linked), out_shape=[o[0] f...]
where the time goes in v4:
time: 189 us; the launch traced here: 188 us
  Pallas kernels  188 us (99%)
    pallas_call x1, Pallas kernels, layer(): pl.pallas_call(functools.partial(layer_kernel, linked), out_shape=[o[0] f...  178 us
    pallas_call x1, Pallas kernels, adam(): pl.pallas_call(adam_kernel, grid=(steps,), out_shape=[jax.ShapeDtypeStruc...  9.98 us

profile of v4, /device:TPU:0, one launch (start us, length us, event | category | flops | bytes accessed | tf_op | source)
XLA Modules:
  0.0 188.4 jit_solution(13275637520285744718)
XLA Ops:
  0.7 177.6 %shard_map.314 = (bf16[1024,768]{1,0:T(8,128)(2,1)}, bf16[1024,768]{1,0:T(8,128)(2,1)}, bf16[4,96,768]{2,1,0:T(8,128)(2,1)}, bf16[4,96,768]{2,1,0:T(8,128)(2,1)}...) custom-call(bf16[1024,768]{1,0:T(8,128)(2,1)} %refs_0_.1, bf16[1024,768]{1,0:T(8,128)(2,1)} %refs_1_.1, ...), custom_call_target="tpu_custom_call" | custom-call | tf_op jit(solution)/shard_map/pallas_call | solution.py:857
  178.2 10.0 %shard_map.315 = (f32[96,2304]{1,0:T(8,128)}, f32[96,768]{1,0:T(8,128)}, f32[96,3072]{1,0:T(8,128)}, f32[384,768]{1,0:T(8,128)}, f32[12,96]{1,0:T(8,128)}, /*ind...) custom-call(bf16[4,96,768]{2,1,0:T(8,128)(2,1)} %get-tuple-element.4, ...), custom_call_target="tpu_custom_call" | custom-call | tf_op jit(solution)/shard_map/pallas_call | solution.py:942

commit v5 on v4

--- a/solution.py
+++ b/solution.py
@@ -21,34 +21,37 @@
 Z_FIRST = (4, 6, 2)
 GATHER_PLAN = {
     "start": {
-        0: [("start", 1), ("plane", 0), ("start", 2), ("plane", 1), ("relay", 0), ("start", 3), ("plane", 2), ("relay", 1), ("last", 0), ("wait", 0)],
+        0: [("plane", 0), ("start", 1), ("relay", 0), ("plane", 1), ("start", 2), ("last", 0), ("wait", 0), ("start", 3)],
     },
     "project0": {
-        1: [("start", 4), ("relay", 2)],
-        2: [("plane", 3), ("last", 1)],
+        1: [("relay", 1)],
+        2: [("plane", 2)],
     },
     "attend0": {
-        0: [("wait", 1), ("last", 2)],
-        2: [("wait", 2), ("start", 5)],
-        3: [("plane", 4), ("relay", 3)],
+        1: [("last", 1)],
+        2: [("start", 4)],
+        3: [("wait", 1), ("relay", 2), ("plane", 3)],
     },
     "attend1": {
+        0: [("last", 2), ("start", 5)],
+        2: [("wait", 2), ("plane", 4)],
+        3: [("relay", 3)],
+    },
+    "project2": {
         2: [("start", 6)],
-        3: [("relay", 4), ("plane", 5)],
-    },
-    "project2": {
-        1: [("last", 3)],
     },
     "attend2": {
-        0: [("wait", 3), ("last", 4)],
-        2: [("wait", 4), ("plane", 6)],
-        3: [("relay", 5)],
+        1: [("plane", 5), ("relay", 4)],
+        3: [("last", 3)],
+    },
+    "out": {
+        1: [("wait", 3)],
+        3: [("plane", 6), ("relay", 5), ("last", 4), ("wait", 4)],
     },
     "up": {
-        0: [("relay", 6)],
-        1: [("last", 5)],
-        2: [("last", 6), ("wait", 5)],
-        3: [("wait", 6)],
+        1: [("relay", 6)],
+        2: [("last", 5)],
+        3: [("last", 6), ("wait", 5), ("wait", 6)],
     },
 }
 SUM_PLAN = {

time: 189 us -> 178 us (0.942)
  Pallas kernels: 188 us -> 177 us
    pallas_call x1, Pallas kernels: 178 us -> 167 us  [layer(): pl.pallas_call(functools.partial(layer_kernel, linked), out_shape=[o[0] f...]
where the time goes in v5:
time: 178 us
  Pallas kernels  177 us (99%)
    pallas_call x1, Pallas kernels, layer(): pl.pallas_call(functools.partial(layer_kernel, linked), out_shape=[o[0] f...  167 us
    pallas_call x1, Pallas kernels, adam(): pl.pallas_call(adam_kernel, grid=(steps,), out_shape=[jax.ShapeDtypeStruc...  9.98 us

profile of v5, /device:TPU:0, one launch (start us, length us, event | category | flops | bytes accessed | tf_op | source)
XLA Modules:
  0.0 178.1 jit_solution(4618031765060544293)
XLA Ops:
  0.7 167.3 %shard_map.314 = (bf16[1024,768]{1,0:T(8,128)(2,1)}, bf16[1024,768]{1,0:T(8,128)(2,1)}, bf16[4,96,768]{2,1,0:T(8,128)(2,1)}, bf16[4,96,768]{2,1,0:T(8,128)(2,1)}...) custom-call(bf16[1024,768]{1,0:T(8,128)(2,1)} %refs_0_.1, bf16[1024,768]{1,0:T(8,128)(2,1)} %refs_1_.1, ...), custom_call_target="tpu_custom_call" | custom-call | tf_op jit(solution)/shard_map/pallas_call | solution.py:860
  168.0 10.0 %shard_map.315 = (f32[96,2304]{1,0:T(8,128)}, f32[96,768]{1,0:T(8,128)}, f32[96,3072]{1,0:T(8,128)}, f32[384,768]{1,0:T(8,128)}, f32[12,96]{1,0:T(8,128)}, /*ind...) custom-call(bf16[4,96,768]{2,1,0:T(8,128)(2,1)} %get-tuple-element.4, ...), custom_call_target="tpu_custom_call" | custom-call | tf_op jit(solution)/shard_map/pallas_call | solution.py:945

commit v6 on v5

--- a/solution.py
+++ b/solution.py
@@ -932,7 +932,7 @@
             copy.wait()
 
 
-def adam(sums, moments, passed, steps=3):
+def adam(sums, moments, passed, steps=2):
     def rows(shape):
         return pl.BlockSpec((shape[0] // steps, shape[1]), lambda i: (i, 0))
 

time: 178 us -> 178 us (level)
  no operation moved by 1% of the time
where the time goes in v6:
time: 178 us
  Pallas kernels  177 us (99%)
    pallas_call x1, Pallas kernels, layer(): pl.pallas_call(functools.partial(layer_kernel, linked), out_shape=[o[0] f...  167 us
    pallas_call x1, Pallas kernels, adam(): pl.pallas_call(adam_kernel, grid=(steps,), out_shape=[jax.ShapeDtypeStruc...  9.59 us

profile of v6, /device:TPU:0, one launch (start us, length us, event | category | flops | bytes accessed | tf_op | source)
XLA Modules:
  0.0 177.7 jit_solution(5355209585352869196)
XLA Ops:
  0.7 167.3 %shard_map.314 = (bf16[1024,768]{1,0:T(8,128)(2,1)}, bf16[1024,768]{1,0:T(8,128)(2,1)}, bf16[4,96,768]{2,1,0:T(8,128)(2,1)}, bf16[4,96,768]{2,1,0:T(8,128)(2,1)}...) custom-call(bf16[1024,768]{1,0:T(8,128)(2,1)} %refs_0_.1, bf16[1024,768]{1,0:T(8,128)(2,1)} %refs_1_.1, ...), custom_call_target="tpu_custom_call" | custom-call | tf_op jit(solution)/shard_map/pallas_call | solution.py:860
  168.0 9.6 %shard_map.315 = (f32[96,2304]{1,0:T(8,128)}, f32[96,768]{1,0:T(8,128)}, f32[96,3072]{1,0:T(8,128)}, f32[384,768]{1,0:T(8,128)}, f32[12,96]{1,0:T(8,128)}, /*ind...) custom-call(bf16[4,96,768]{2,1,0:T(8,128)(2,1)} %get-tuple-element.4, ...), custom_call_target="tpu_custom_call" | custom-call | tf_op jit(solution)/shard_map/pallas_call | solution.py:945
